TPU v7x, 32 devices: a whole 2x2x4 slice. The times are simulated.
32 devices in a mesh: item: 2 (over x), tok: 16 (over z, y, core).
Axes of the slice: x: 2, y: 2, z: 4, core: 2. Of those that a mesh axis runs over, the one named last changes fastest.
Arguments:
- tokens: bfloat16 [4, 2048, 1024], P('item', 'tok'), may hold values from -6 to 6
- norm_gain: bfloat16 [1024], P(('item', 'tok')), may hold values from 0.5 to 1.5
- norm_shift: bfloat16 [1024], P(('item', 'tok')), may hold values from -3 to 3
- w_up: bfloat16 [1024, 3072], P(('item', 'tok')), may hold values from -0.1875 to 0.1875
- w_value: bfloat16 [1024, 512], P(('item', 'tok')), may hold values from -0.1875 to 0.1875
- w_back: bfloat16 [512, 3072], P(('item', 'tok')), may hold values from -0.25 to 0.25
- w_down: bfloat16 [3072, 1024], P(('item', 'tok')), may hold values from -0.21875 to 0.21875
- mode_coef: bfloat16 [512, 1024], P('tok', 'item'), may hold values from -0.015625 to 0.015625
- skip_gain: bfloat16 [512], P('tok'), may hold values from -3 to 3
- cotangent: bfloat16 [4, 2048, 1024], P('item', 'tok'), may hold values from -6 to 6
Outputs:
- result: bfloat16 [4, 2048, 1024], P('item', 'tok')
- grad_tokens: float32 [4, 2048, 1024], P('item', 'tok')
- grad_norm_gain: float32 [1024], P(('item', 'tok'))
- grad_norm_shift: float32 [1024], P(('item', 'tok'))
- grad_w_up: float32 [1024, 3072], P(('item', 'tok'))
- grad_w_value: float32 [1024, 512], P(('item', 'tok'))
- grad_w_back: float32 [512, 3072], P(('item', 'tok'))
- grad_w_down: float32 [3072, 1024], P(('item', 'tok'))
- grad_mode_coef: float32 [512, 1024], P('tok', 'item')
- grad_skip_gain: float32 [512], P('tok')
All inputs are finite; a program needn't handle non-finite values.
Results may differ from a plain program's by a relative error of at most 0.0082.
Values may be sent and summed in bfloat16 or wider, within the bound.
A program may use at most 192 MiB of HBM per device.

v0:
```python
import math

import jax
import jax.numpy as jnp
from jax import lax
from jax.sharding import PartitionSpec as P

highest = lax.Precision.HIGHEST


def basis_block(start_index, block_width, length, states):
    places = start_index + jnp.arange(block_width, dtype=jnp.int32)
    mode_ids = jnp.arange(states, dtype=jnp.int32)
    fraction = (mode_ids * 41 % states).astype(jnp.float32) / states
    mode_rates = jnp.exp(jnp.log(1.0 / 32.0) + fraction * jnp.log(32.0 / (4.0 * length)))
    decays = jnp.exp(-mode_rates[:, None] * places[None, :].astype(jnp.float32))
    phase_turns = (mode_ids[:, None] * places[None, :] % (2 * states)).astype(jnp.float32) * (
        jnp.pi / states
    )
    return jnp.concatenate([decays * jnp.cos(phase_turns), decays * jnp.sin(phase_turns)], axis=0)


def make_kernel(coef_full, length):
    states = coef_full.shape[1] // 2
    block_width = math.gcd(length, 2048)
    block_count = length // block_width

    def one_block(block_index):
        table = basis_block(block_index * block_width, block_width, length, states)
        return jnp.dot(coef_full, table, precision=highest)

    pieces = lax.map(one_block, jnp.arange(block_count, dtype=jnp.int32))
    return jnp.transpose(pieces, (1, 0, 2)).reshape(coef_full.shape[0], length)


def coef_gradient(grad_kernel, states):
    channels, length = grad_kernel.shape
    block_width = math.gcd(length, 2048)
    block_count = length // block_width
    slabs = grad_kernel.reshape(channels, block_count, block_width)

    def add_block(running, block_index):
        slab_part = lax.dynamic_index_in_dim(slabs, block_index, 1, keepdims=False)
        table = basis_block(block_index * block_width, block_width, length, states)
        return (running + jnp.dot(slab_part, table.T, precision=highest), None)

    start_total = jnp.zeros((channels, 2 * states), jnp.float32)
    summed, unused = lax.scan(add_block, start_total, jnp.arange(block_count, dtype=jnp.int32))
    return summed


def unit_tables(row_count, column_count, period):
    row_ids = jnp.arange(row_count, dtype=jnp.int32)[:, None]
    column_ids = jnp.arange(column_count, dtype=jnp.int32)[None, :]
    phase_turns = (row_ids * column_ids % period).astype(jnp.float32) * (2.0 * jnp.pi / period)
    return (jnp.cos(phase_turns), jnp.sin(phase_turns))


def right_product(left_part, table):
    return jnp.einsum("...kq,qm->...km", left_part, table, precision=highest)


def spectrum(signal):
    length = signal.shape[-1]
    padded_size = 2 * length
    outer_size = padded_size // 128
    half_size = outer_size // 2
    folded = signal.reshape(signal.shape[:-1] + (half_size, 128))
    cos_outer, sin_outer = unit_tables(outer_size, half_size, outer_size)
    section_real = jnp.einsum("kp,...pq->...kq", cos_outer, folded, precision=highest)
    section_imag = -jnp.einsum("kp,...pq->...kq", sin_outer, folded, precision=highest)
    twist_cos, twist_sin = unit_tables(outer_size, 128, padded_size)
    turned_real = section_real * twist_cos + section_imag * twist_sin
    turned_imag = section_imag * twist_cos - section_real * twist_sin
    cos_inner, sin_inner = unit_tables(128, 128, 128)
    out_real = right_product(turned_real, cos_inner) + right_product(turned_imag, sin_inner)
    out_imag = right_product(turned_imag, cos_inner) - right_product(turned_real, sin_inner)
    return (out_real, out_imag)


def inverse(spec_real, spec_imag):
    outer_size = spec_real.shape[-2]
    padded_size = outer_size * 128
    half_size = outer_size // 2
    cos_inner, sin_inner = unit_tables(128, 128, 128)
    back_real = right_product(spec_real, cos_inner) - right_product(spec_imag, sin_inner)
    back_imag = right_product(spec_real, sin_inner) + right_product(spec_imag, cos_inner)
    twist_cos, twist_sin = unit_tables(outer_size, 128, padded_size)
    turned_real = back_real * twist_cos - back_imag * twist_sin
    turned_imag = back_real * twist_sin + back_imag * twist_cos
    cos_outer, sin_outer = unit_tables(half_size, outer_size, outer_size)
    signal = jnp.einsum("pk,...kq->...pq", cos_outer, turned_real, precision=highest)
    signal = signal - jnp.einsum("pk,...kq->...pq", sin_outer, turned_imag, precision=highest)
    return signal.reshape(signal.shape[:-2] + (half_size * 128,)) / padded_size


def layer_norm(token_rows, gain_row, shift_row):
    row_mean = jnp.mean(token_rows, axis=-1, keepdims=True)
    centered = token_rows - row_mean
    variance = jnp.mean(centered * centered, axis=-1, keepdims=True)
    return centered * lax.rsqrt(variance + 1e-05) * gain_row + shift_row


def body(
    tokens, norm_gain, norm_shift, w_up, w_value, w_back, w_down, mode_coef, skip_gain, cotangent
):
    gain_full, shift_full, up_full, value_full = (
        lax.all_gather(norm_gain, ("item", "tok"), axis=0, tiled=True),
        lax.all_gather(norm_shift, ("item", "tok"), axis=0, tiled=True),
        lax.all_gather(w_up, ("item", "tok"), axis=0, tiled=True),
        lax.all_gather(w_value, ("item", "tok"), axis=0, tiled=True),
    )
    back_full, down_full = (
        lax.all_gather(w_back, ("item", "tok"), axis=0, tiled=True),
        lax.all_gather(w_down, ("item", "tok"), axis=0, tiled=True),
    )
    coef_full = lax.all_gather(mode_coef, "item", axis=1, tiled=True)
    token_rows = tokens.astype(jnp.float32)
    gain_float = gain_full.astype(jnp.float32)
    shift_float = shift_full.astype(jnp.float32)
    normed = layer_norm(token_rows, gain_float, shift_float).astype(jnp.bfloat16)
    up_pre = jnp.einsum("std,df->stf", normed, up_full, preferred_element_type=jnp.float32)
    value_pre = jnp.einsum("std,dh->sht", normed, value_full, preferred_element_type=jnp.float32)
    value = jax.nn.gelu(value_pre).astype(jnp.bfloat16)
    channel_values = lax.all_to_all(value, "tok", split_axis=1, concat_axis=2, tiled=True)
    length = channel_values.shape[-1]
    kernel = make_kernel(coef_full.astype(jnp.float32), length)
    signal = channel_values.astype(jnp.float32)
    skip_column = skip_gain.astype(jnp.float32)[:, None]
    value_real, value_imag = spectrum(signal)
    kernel_real, kernel_imag = spectrum(kernel)
    conv_out = inverse(
        value_real * kernel_real - value_imag * kernel_imag,
        value_real * kernel_imag + value_imag * kernel_real,
    )
    mixed_channels = (conv_out + skip_column * signal).astype(jnp.bfloat16)
    mixed = lax.all_to_all(mixed_channels, "tok", split_axis=2, concat_axis=1, tiled=True)
    gate = jnp.einsum("sht,hf->stf", mixed, back_full, preferred_element_type=jnp.float32)
    up_act = jax.nn.gelu(up_pre)
    hidden = (up_act * gate).astype(jnp.bfloat16)
    branch = jnp.einsum("stf,fd->std", hidden, down_full, preferred_element_type=jnp.float32)
    result = (token_rows + branch).astype(jnp.bfloat16)
    grad_w_down = jnp.einsum("stf,std->fd", hidden, cotangent, preferred_element_type=jnp.float32)
    grad_hidden = jnp.einsum(
        "std,fd->stf", cotangent, down_full, preferred_element_type=jnp.float32
    )
    grad_gate = (grad_hidden * up_act).astype(jnp.bfloat16)
    grad_up_act = grad_hidden * gate
    grad_w_back = jnp.einsum("sht,stf->hf", mixed, grad_gate, preferred_element_type=jnp.float32)
    grad_mixed = jnp.einsum(
        "stf,hf->sht", grad_gate, back_full, preferred_element_type=jnp.float32
    ).astype(jnp.bfloat16)
    grad_channels = lax.all_to_all(grad_mixed, "tok", split_axis=1, concat_axis=2, tiled=True)
    grad_signal = grad_channels.astype(jnp.float32)
    grad_real, grad_imag = spectrum(grad_signal)
    grad_value_channels = inverse(
        kernel_real * grad_real + kernel_imag * grad_imag,
        kernel_real * grad_imag - kernel_imag * grad_real,
    )
    grad_value_channels = (grad_value_channels + skip_column * grad_signal).astype(jnp.bfloat16)
    grad_kernel = inverse(
        jnp.sum(grad_real * value_real + grad_imag * value_imag, axis=0),
        jnp.sum(grad_imag * value_real - grad_real * value_imag, axis=0),
    )
    grad_skip_part = jnp.sum(grad_signal * signal, axis=(0, 2))
    grad_coef_part = coef_gradient(grad_kernel, coef_full.shape[1] // 2)
    grad_mode_coef = lax.psum_scatter(grad_coef_part, "item", scatter_dimension=1, tiled=True)
    grad_skip_gain = lax.psum(grad_skip_part, "item")
    grad_value = lax.all_to_all(grad_value_channels, "tok", split_axis=2, concat_axis=1, tiled=True)
    gelu_value_back = jax.vjp(jax.nn.gelu, value_pre)[1]
    grad_value_pre = gelu_value_back(grad_value.astype(jnp.float32))[0].astype(jnp.bfloat16)
    gelu_up_back = jax.vjp(jax.nn.gelu, up_pre)[1]
    grad_up_pre = gelu_up_back(grad_up_act)[0].astype(jnp.bfloat16)
    grad_w_up = jnp.einsum("std,stf->df", normed, grad_up_pre, preferred_element_type=jnp.float32)
    grad_w_value = jnp.einsum(
        "std,sht->dh", normed, grad_value_pre, preferred_element_type=jnp.float32
    )
    grad_normed = jnp.einsum(
        "stf,df->std", grad_up_pre, up_full, preferred_element_type=jnp.float32
    )
    grad_normed = grad_normed + jnp.einsum(
        "sht,dh->std", grad_value_pre, value_full, preferred_element_type=jnp.float32
    )
    norm_back = jax.vjp(layer_norm, token_rows, gain_float, shift_float)[1]
    grad_rows, grad_gain_part, grad_shift_part = norm_back(grad_normed)
    grad_tokens = cotangent.astype(jnp.float32) + grad_rows
    owners = lax.axis_size("item") * lax.axis_size("tok")
    norm_flat = jnp.concatenate(
        [grad_gain_part.reshape(owners, -1), grad_shift_part.reshape(owners, -1)], axis=1
    )
    up_flat = grad_w_up.reshape(owners, -1)
    value_flat = grad_w_value.reshape(owners, -1)
    back_flat = grad_w_back.reshape(owners, -1)
    down_flat = grad_w_down.reshape(owners, -1)
    summed = (
        lax.psum_scatter(norm_flat, ("item", "tok"), scatter_dimension=0, tiled=True),
        lax.psum_scatter(up_flat, ("item", "tok"), scatter_dimension=0, tiled=True),
        lax.psum_scatter(value_flat, ("item", "tok"), scatter_dimension=0, tiled=True),
        lax.psum_scatter(back_flat, ("item", "tok"), scatter_dimension=0, tiled=True),
        lax.psum_scatter(down_flat, ("item", "tok"), scatter_dimension=0, tiled=True),
    )
    gain_count = norm_gain.shape[0]
    norm_row = summed[0].reshape(-1)
    grad_norm_gain = norm_row[:gain_count]
    grad_norm_shift = norm_row[gain_count:]
    grad_up_out = summed[1].reshape(w_up.shape)
    grad_value_out = summed[2].reshape(w_value.shape)
    grad_back_out = summed[3].reshape(w_back.shape)
    grad_down_out = summed[4].reshape(w_down.shape)
    return (
        result,
        grad_tokens,
        grad_norm_gain,
        grad_norm_shift,
        grad_up_out,
        grad_value_out,
        grad_back_out,
        grad_down_out,
        grad_mode_coef,
        grad_skip_gain,
    )


def solution(mesh):
    in_specs = (
        P("item", "tok", None),
        P(("item", "tok")),
        P(("item", "tok")),
        P(("item", "tok"), None),
        P(("item", "tok"), None),
        P(("item", "tok"), None),
        P(("item", "tok"), None),
        P("tok", "item"),
        P("tok"),
        P("item", "tok", None),
    )
    out_specs = (
        P("item", "tok", None),
        P("item", "tok", None),
        P(("item", "tok")),
        P(("item", "tok")),
        P(("item", "tok"), None),
        P(("item", "tok"), None),
        P(("item", "tok"), None),
        P(("item", "tok"), None),
        P("tok", "item"),
        P("tok"),
    )
    return jax.shard_map(body, mesh=mesh, in_specs=in_specs, out_specs=out_specs, check_vma=False)
```

profile of v0, /device:TPU:0, one launch (start us, length us, event | category | flops | bytes accessed | tf_op | source)
XLA Modules:
  0.0 905.0 jit_solution(4486735189626205670)
XLA Ops:
  12.3 42.0 %all-reduce.8 = (bf16[1024]{0:T(1024)(128)(2,1)S(1)}, bf16[1024]{0:T(1024)(128)(2,1)S(1)}) all-reduce(bf16[1024]{0:T(1024)(128)(2,1)S(1)} %dynamic-update-slice.1, bf16[1024]{0:T(1024)(128)(2,1)S(1)} %dynamic-update-slice), channel_id=1, replica_groups=mesh['item'=2,'tok'=16] {'item','tok'}, use_global_device_ids=true, to_apply=%add.1 | all-reduce | flops 2048 | bytes 8192
  54.3 5.1 all_gather.25
  59.5 17.5 %cosine_multiply_fusion = (f32[512,2048]{1,0:T(8,128)S(1)}, f32[512,2048]{1,0:T(8,128)S(1)}) fusion(f32[2048]{0:T(1024)S(1)} %iota_convert_fusion, f32[512]{0:T(512)S(1)} %fusion.232), kind=kLoop, calls=%fused_computation.23 | loop fusion | flops 17825792 | bytes 8398848 | tf_op jit(solution)/shard_map/while/body/eval_jaxpr/mul | solution.py:20
  87.4 5.6 all-to-all-start
  94.6 10.7 %all-to-all-done = bf16[2,512,128]{2,0,1:T(2,128)(2,1)S(1)} async-done(((bf16[2,512,128]{2,0,1:T(2,128)(2,1)}), bf16[2,512,128]{2,0,1:T(2,128)(2,1)S(1)}, u32[]{:S(2)}, u32[]{:S(2)}) %all-to-all-start) | async-done | bytes 262176 | tf_op jit(solution)/shard_map/all_to_all | solution.py:125
  131.8 14.2 %all_to_all.57 = bf16[16,2,4096]{2,1,0:T(2,128)(2,1)} all-to-all(bf16[16,2,4096]{2,1,0:T(2,128)(2,1)} %reshape.274), channel_id=1, replica_groups=mesh['item'=2,'tok'=16] {'tok'}, dimensions={0} | all-to-all | bytes 524288 | tf_op jit(solution)/shard_map/all_to_all | solution.py:137
  153.2 4.7 fusion.25
  157.9 43.9 %all-gather.5.cloned.1.call-done = bf16[1024,3072]{1,0:T(8,128)(2,1)} async-done(((bf16[32,3072]{1,0:T(8,128)(2,1)}), bf16[1024,3072]{1,0:T(8,128)(2,1)}) %all-gather.5.cloned.1.call-update) | async-done | bytes 6291472 | tf_op jit(solution)/shard_map/all_gather | solution.py:110
  201.7 6.5 fusion.8
  208.2 64.3 %all-gather.11.cloned.1.call-done = bf16[3072,1024]{1,0:T(8,128)(2,1)} async-done(((bf16[96,1024]{1,0:T(8,128)(2,1)}), bf16[3072,1024]{1,0:T(8,128)(2,1)}) %all-gather.11.cloned.1.call-update) | async-done | bytes 6291472 | tf_op jit(solution)/shard_map/all_gather | solution.py:115
  272.6 10.5 %multiply_convert_fusion = (bf16[2,128,3072]{2,1,0:T(8,128)(2,1)S(1)}, bf16[2,128,3072]{2,1,0:T(8,128)(2,1)}, bf16[2,128,3072]{2,1,0:T(8,128)(2,1)}) fusion(f32[2,128,3072]{2,1,0:T(8,128)} %fusion.8, f32[2,128,3072]{2,1,0:T(8,128)} %fusion.25, bf16[2,128,1024]{2,1,0:T(8,128)(2,1)} %param.19, bf16[3072,1024]{1,0:T(8,128)(2,1)} %all-gather.11.cloned.1.call-done), kind=kOutput, calls=%fused_computation.39 | convolution fusion | flops 1631059968 | bytes 17825792 | tf_op jit(solution)/shard_map/std,fd->stf/dot_general | solution.py:144
  292.0 5.1 convolution_bitcast_fusion.2
  297.2 6.6 reshape.220
  333.3 5.9 all-to-all-start.3
  339.4 6.5 convolution_bitcast_fusion.1
  345.8 10.0 %reshape.216 = f32[32,98304]{1,0:T(8,128)} reshape(f32[1024,3072]{1,0:T(8,128)} %convolution_bitcast_fusion.1) | data formatting | bytes 25165824 | tf_op jit(solution)/shard_map/reshape | solution.py:191
  355.9 6.4 convolution_bitcast_fusion
  362.3 9.8 %reshape.222 = f32[32,98304]{1,0:T(8,128)} reshape(f32[3072,1024]{1,0:T(8,128)} %convolution_bitcast_fusion) | data formatting | bytes 25165824 | tf_op jit(solution)/shard_map/reshape | solution.py:194
  380.4 5.7 fusion.6
  386.1 5.9 fusion.35
  393.3 5.7 psum.7
  403.4 10.2 %fusion = f32[32,1024]{1,0:T(8,128)} fusion(f32[512,2048]{1,0:T(8,128)} %copy-done.2, f32[512,2048]{1,0:T(8,128)S(1)} %copy-done.1, f32[4,8,16,128]{3,2,1,0:T(8,128)S(1)} %bitcast.251), kind=kOutput, calls=%fused_computation.1 | convolution fusion | flops 807403520 | bytes 8781824 | tf_op jit(solution)/shard_map/while/body/eval_jaxpr/dot_general | solution.py:45
  417.8 42.3 %all-reduce.2 = f32[32,64]{1,0:T(8,128)S(1)} all-reduce(f32[32,64]{1,0:T(8,128)S(1)} %pad_maximum_fusion.5), channel_id=2, replica_groups=mesh['item'=2,'tok'=16] {'item','tok'}, use_global_device_ids=true, to_apply=%region_6.7.clone | all-reduce | flops 2048 | bytes 16384
  460.7 424.4 %all-reduce.11.cloned.1.call-done = (f32[32,98304]{1,0:T(8,128)}, f32[32,16384]{1,0:T(8,128)}, f32[32,49152]{1,0:T(8,128)}, f32[32,98304]{1,0:T(8,128)}) async-done(((f32[32,98304]{1,0:T(8,128)}, f32[32,16384]{1,0:T(8,128)}, f32[32,49152]{1,0:T(8,128)}, f32[32,98304]{1,0:T(8,128)}), (f32[32,98304]{1,0:T(8,128)}, f32[32,16384]{1,0:T(8,128)}, f32[32,49152]{1,0:T(8,128)}, ...) | async-done | bytes 33554448
  (162 shorter events, 120.1 us)
Async XLA Ops:
  7.2 76.8 %all-gather.7.cloned.1.call-start = ((), (), s32[]{:S(2)}) async-start(), calls=%async_computation.6 | async-start | bytes 1081344 | tf_op jit(solution)/shard_map/all_gather | solution.py:111
  7.9 145.3 %all-gather.9.cloned.1.call-start = ((), (), s32[]{:S(2)}) async-start(), calls=%async_computation.7 | async-start | bytes 3244032 | tf_op jit(solution)/shard_map/all_gather | solution.py:114
  8.7 193.1 %all-gather.5.cloned.1.call-start = ((), (), s32[]{:S(2)}) async-start(), calls=%async_computation.5 | async-start | bytes 6488064 | tf_op jit(solution)/shard_map/all_gather | solution.py:110
  9.4 263.2 %all-gather.11.cloned.1.call-start = ((), (), s32[]{:S(2)}) async-start(), calls=%async_computation.8 | async-start | bytes 6488064 | tf_op jit(solution)/shard_map/all_gather | solution.py:115
  77.0 3.3 copy-start
  77.0 3.4 copy-start.7
  87.4 17.9 %all-to-all-start = ((bf16[2,512,128]{2,0,1:T(2,128)(2,1)}), bf16[2,512,128]{2,0,1:T(2,128)(2,1)S(1)}, u32[]{:S(2)}, u32[]{:S(2)}) async-start(bf16[2,512,128]{2,0,1:T(2,128)(2,1)} %copy.73), calls=%async_computation | async-start | bytes 524288 | tf_op jit(solution)/shard_map/all_to_all | solution.py:125
  272.6 11.7 %copy-start.12 = (bf16[512,3072]{1,0:T(8,128)(2,1)S(1)}, bf16[512,3072]{1,0:T(8,128)(2,1)}, u32[]{:S(2)}) copy-start(bf16[512,3072]{1,0:T(8,128)(2,1)} %all-gather.9.cloned.1.call-done) | copy-start | bytes 9437188
  287.8 16.0 %all-to-all-start.2 = ((bf16[2,512,128]{2,0,1:T(2,128)(2,1)}), bf16[2,512,128]{2,0,1:T(2,128)(2,1)}, u32[]{:S(2)}, u32[]{:S(2)}) async-start(bf16[2,512,128]{2,0,1:T(2,128)(2,1)} %copy.80), calls=%async_computation.2 | async-start | bytes 524288 | tf_op jit(solution)/shard_map/all_to_all | solution.py:153
  312.8 4.8 copy-start.3
  319.9 5.3 copy-start.4
  320.0 5.3 copy-start.6
  328.4 11.0 %copy-start.8 = (bf16[2,128,1024]{2,1,0:T(8,128)(2,1)S(1)}, bf16[2,128,1024]{2,1,0:T(8,128)(2,1)}, u32[]{:S(2)}) copy-start(bf16[2,128,1024]{2,1,0:T(8,128)(2,1)} %param.10) | copy-start | bytes 1572868
  329.3 10.0 %copy-start.18 = (bf16[2,128,3072]{2,1,0:T(8,128)(2,1)S(1)}, bf16[2,128,3072]{2,1,0:T(8,128)(2,1)}, u32[]{:S(2)}) copy-start(bf16[2,128,3072]{2,1,0:T(8,128)(2,1)} %get-tuple-element.40) | copy-start | bytes 4718596
  333.3 38.8 %all-to-all-start.3 = ((bf16[16,2,4096]{2,1,0:T(2,128)(2,1)}), bf16[16,2,4096]{2,1,0:T(2,128)(2,1)}, u32[]{:S(2)}, u32[]{:S(2)}) async-start(bf16[16,2,4096]{2,1,0:T(2,128)(2,1)} %reshape.276), calls=%async_computation.3 | async-start | bytes 524288 | tf_op jit(solution)/shard_map/all_to_all | solution.py:169
  339.3 545.8 %all-reduce.11.cloned.1.call-start = ((), (), s32[]{:S(2)}) async-start(), calls=%async_computation.10 | async-start | bytes 67108864
  345.8 10.1 %copy-start.14 = (bf16[2,128,1024]{2,1,0:T(8,128)(2,1)S(1)}, bf16[2,128,1024]{2,1,0:T(8,128)(2,1)}, u32[]{:S(2)}) copy-start(bf16[2,128,1024]{2,1,0:T(8,128)(2,1)} %param.19) | copy-start | bytes 1572868
  345.8 10.1 %copy-start.16 = (bf16[2,128,3072]{2,1,0:T(8,128)(2,1)S(1)}, bf16[2,128,3072]{2,1,0:T(8,128)(2,1)}, u32[]{:S(2)}) copy-start(bf16[2,128,3072]{2,1,0:T(8,128)(2,1)} %get-tuple-element.41) | copy-start | bytes 4718596
  372.2 4.3 copy-start.22
  379.0 518.7 %reduce-scatter.2.cloned.1.call-start = ((), (), s32[]{:S(2)}) async-start(), calls=%async_computation.9 | async-start | bytes 196608 | tf_op jit(solution)/shard_map/reduce_scatter | solution.py:167
  380.4 5.7 copy-start.17
  386.1 12.9 %copy-start.10 = (f32[32,32,128]{2,1,0:T(8,128)S(1)}, f32[32,32,128]{2,1,0:T(8,128)}, u32[]{:S(2)}) copy-start(f32[32,32,128]{2,1,0:T(8,128)} %get-tuple-element.29) | copy-start | bytes 1572868
  386.1 14.6 %copy-start.9 = (f32[32,32,128]{2,1,0:T(8,128)S(1)}, f32[32,32,128]{2,1,0:T(8,128)}, u32[]{:S(2)}) copy-start(f32[32,32,128]{2,1,0:T(8,128)} %get-tuple-element.28) | copy-start | bytes 1572868
  403.4 10.3 %copy-start.21 = (bf16[1024,512]{1,0:T(8,128)(2,1)S(1)}, bf16[1024,512]{1,0:T(8,128)(2,1)}, u32[]{:S(2)}) copy-start(bf16[1024,512]{1,0:T(8,128)(2,1)} %all-gather.7.cloned.1.call-done) | copy-start | bytes 3145732
  (8 other events, 18.3 us)
Sparse Core Ops, SparseCore 0:
  10.9 56.5 all-gather.6
  70.3 60.0 all-gather.8
  133.3 68.3 all-gather.4
  204.5 68.0 all-gather.10
  379.1 505.9 all-reduce.10
  887.8 9.8 reduce-scatter.1
where the time goes:
time: 914 us; the launch traced here: 905 us
  waiting for transfers between devices  547 us (60%)
  matrix products  115 us (13%)
  blocking collectives  109 us (12%)
  local copies, waits for them, and re-layouts  75.2 us (8%)
  other arithmetic  27.5 us (3%)
  starting transfers between devices  16.2 us (2%)
  between operations  15.2 us (2%)
    unnamed x7, waiting for transfers between devices  427 us
    unnamed x2, blocking collectives  84.3 us
    all_gather x1, waiting for transfers between devices, body(): lax.all_gather(w_down, ('item', 'tok'), axis=0, tiled=True)  64.3 us
    all_gather x1, waiting for transfers between devices, body(): lax.all_gather(w_up, ('item', 'tok'), axis=0, tiled=True)  43.9 us
    dot_general x24, matrix products, right_product(): return jnp.einsum('...kq,qm->...km', left_part, table, precision=highest)  32.1 us
    unnamed x61, local copies, waits for them, and re-layouts  25.5 us
  transfers between devices with their start and end apart: 9, of which 5 were waited for; matrix products, arithmetic and copies ran while one was open for 18% of the time, Pallas kernels for 0%

commit v1 on v0

--- a/solution.py
+++ b/solution.py
@@ -1,8 +1,14 @@
+import functools
 import math
+import types
 
 import jax
 import jax.numpy as jnp
+import ml_dtypes
+import numpy as np
 from jax import lax
+from jax.experimental import pallas as pl
+from jax.experimental.pallas import tpu as pltpu
 from jax.sharding import PartitionSpec as P
 
 highest = lax.Precision.HIGHEST
@@ -221,6 +227,1026 @@
     )
 
 
+MESH_ID = pl.DeviceIdType.MESH
+bf16, f32 = jnp.bfloat16, jnp.float32
+NT = (((1,), (1,)), ((), ()))
+GC = math.sqrt(2.0 / math.pi)
+
+
+def dot(a, b):
+    return jnp.dot(a, b, preferred_element_type=f32)
+
+
+def dot_nt(a, b):
+    return lax.dot_general(a, b, NT, preferred_element_type=f32)
+
+
+def gelu_parts(v):
+    t = jnp.tanh(GC * (v + 0.044715 * v * v * v))
+    half = 0.5 * (1.0 + t)
+    slope = half + 0.5 * v * (1.0 - t * t) * (GC * (1.0 + 3 * 0.044715 * v * v))
+    return v * half, slope
+
+
+def split(v):
+    high = v.astype(bf16)
+    return high, (v - high.astype(f32)).astype(bf16)
+
+
+def mode_tables(states, length):
+    n = np.arange(states)
+    rates = np.exp(np.log(1.0 / 32.0) + (n * 41 % states) / states * np.log(32.0 / (4.0 * length)))
+
+    def table(places):
+        decay = np.exp(-rates[:, None] * places[None, :])
+        turn = (n[:, None] * places[None, :] % (2 * states)) * (np.pi / states)
+        return decay * np.cos(turn), decay * np.sin(turn)
+
+    far_re, far_im = table(np.arange(0, length, 128))
+    near = np.concatenate(table(np.arange(128)), axis=0).astype(np.float32)
+    high = near.astype(ml_dtypes.bfloat16)
+    low = (near - high.astype(np.float32)).astype(ml_dtypes.bfloat16)
+    return (
+        far_re.T.astype(np.float32).copy(),
+        far_im.T.astype(np.float32).copy(),
+        high,
+        low,
+        high.T.copy(),
+        low.T.copy(),
+    )
+
+
+class Links:
+    def __init__(self, send_sems, recv_sems, place):
+        self.send_sems, self.recv_sems, self.place = send_sems, recv_sems, place
+        self.count = 0
+        self.pending = []
+
+    def take(self, n=1):
+        first = self.count
+        self.count += n
+        return first
+
+    def make(self, src, dst, ssem, rsem, to):
+        return pltpu.make_async_remote_copy(
+            src_ref=src,
+            dst_ref=dst,
+            send_sem=self.send_sems.at[ssem],
+            recv_sem=self.recv_sems.at[rsem],
+            device_id=to,
+            device_id_type=MESH_ID,
+        )
+
+    def put(self, src, dst, to):
+        slot = self.take()
+        copy = self.make(src, dst, slot, slot, to)
+        copy.start()
+        self.pending.append((copy, None))
+        return slot
+
+    def got(self, slot, region):
+        self.make(region, region, slot, slot, self.place).wait_recv()
+
+    def put_or_keep(self, src, dst, ssem, rsem, to, here):
+        remote = self.make(src, dst, ssem, rsem, to)
+        local = pltpu.make_async_copy(src, dst, self.recv_sems.at[rsem])
+        away = jnp.logical_not(here)
+        pl.when(here)(local.start)
+        pl.when(away)(remote.start)
+        self.pending.append((remote, away))
+
+    def finish(self):
+        for copy, away in self.pending:
+            if away is None:
+                copy.wait_send()
+            else:
+                pl.when(away)(copy.wait_send)
+
+
+N_SEMS = 200
+
+
+def layer_kernel(names, *refs):
+    r_ = dict(zip(names, refs))
+    g = types.SimpleNamespace(**r_)
+    x = lax.axis_index("item")
+    tok = lax.axis_index("tok")
+    z, y, c = tok // 4, (tok // 2) % 2, tok % 2
+    n = tok // 2
+    r = 2 * x + c
+
+    def dev(x_, z_, y_, c_):
+        return (x_, z_ * 4 + y_ * 2 + c_)
+
+    def zo(k):
+        return lax.rem(z + k, 4)
+
+    def zb(k):
+        return lax.rem(z + 4 - k, 4)
+
+    def node(z_, y_):
+        return 2 * z_ + y_
+
+    sib, xn, diag = dev(x, z, y, 1 - c), dev(1 - x, z, y, c), dev(1 - x, z, y, 1 - c)
+    r_sib, r_xn, r_diag = 2 * x + 1 - c, 2 * (1 - x) + c, 2 * (1 - x) + 1 - c
+    members = ((sib, x, 1 - c, r_sib), (xn, 1 - x, c, r_xn), (diag, 1 - x, 1 - c, r_diag))
+    ynb = dev(x, z, 1 - y, c)
+    lk = Links(g.ssem, g.rsem, ynb)
+    aligned = pl.multiple_of
+
+    barrier = pltpu.get_barrier_semaphore()
+    partners = [m[0] for m in members]
+    for k in range(1, 4):
+        partners += [dev(x, zo(k), y, c), dev(x, zo(k), 1 - y, c), dev(x, zo(k), y, 1 - c)]
+    partners.append(ynb)
+    for p in partners:
+        pl.semaphore_signal(barrier, inc=1, device_id=p, device_id_type=MESH_ID)
+
+    eye = lax.broadcasted_iota(jnp.int32, (32, 128), 0) == lax.broadcasted_iota(
+        jnp.int32, (32, 128), 1
+    )
+    eye = eye.astype(bf16)
+    ch_i = lax.broadcasted_iota(jnp.int32, (512, 128), 0)
+    p_i = lax.broadcasted_iota(jnp.int32, (512, 128), 1)
+    row16 = lax.broadcasted_iota(jnp.int32, (16, 128), 0)
+    gain_row = dot(g.norm_gain[...], eye)
+    shift_row = dot(g.norm_shift[...], eye)
+    norm_pack = jnp.where(
+        row16 == 0,
+        jnp.broadcast_to(gain_row, (16, 128)),
+        jnp.where(row16 == 1, jnp.broadcast_to(shift_row, (16, 128)), 0.0),
+    ).astype(bf16)
+    for rr in range(4):
+        pick = ch_i == 64 * (p_i // 16) + 32 * (rr % 2) + 16 * (rr // 2) + p_i % 16
+        pick = pick.astype(bf16)
+        g.perm[:, 128 * rr : 128 * rr + 128] = pick
+        g.pk_send[rr, 0:32, :] = dot(g.w_value[...], pick).astype(bf16)
+        g.pk_send[rr, 32:48, :] = norm_pack
+    pl.semaphore_wait(barrier, len(partners))
+
+    pk_s, up_s, back_s = [], [], []
+    for to, xm, cm, rm in members:
+        pk_s.append(lk.put(g.pk_send.at[rm], g.pk.at[x, n, c], to))
+    coef_s = lk.put(g.mode_coef.at[pl.ds(aligned(16 * (1 - x), 16), 16), :], g.coef.at[x], xn)
+    my_back = g.w_back_all.at[c, y, x, z]
+
+    def cols(rm):
+        return pl.ds(aligned(768 * rm, 128), 768)
+
+    for to, xm, cm, rm in members:
+        up_s.append(lk.put(g.w_up.at[:, cols(rm)], g.w_up_all.at[x, n, c], to))
+    for to, xm, cm, rm in members:
+        back_s.append(lk.put(g.w_back.at[:, cols(rm)], my_back, to))
+    tok_sib = lk.put(g.tokens, g.tok_all.at[r], sib)
+    tok_x = lk.put(g.tokens, g.tok_all.at[r], xn)
+    cot_sib = lk.put(g.cot, g.cot_all.at[r], sib)
+    cot_x = lk.put(g.cot, g.cot_all.at[r], xn)
+    g.pk[x, n, c] = g.pk_send[r]
+    g.w_up_all[x, n, c] = g.w_up[:, cols(r)]
+    g.w_back_all[c, y, x, z] = g.w_back[:, cols(r)]
+    g.cot_all[r] = g.cot[...]
+    g.coef[x] = g.mode_coef[pl.ds(aligned(16 * x, 16), 16), :]
+
+    def gather_start(region):
+        slots = {}
+        for k in (1, 2, 3):
+            slots[k] = lk.put(region(z, y), region(z, y), dev(x, zo(k), y, c))
+        slots[4] = lk.put(region(z, y), region(z, y), ynb)
+        return slots
+
+    def gather_pass(slots, region, k):
+        lk.got(slots[k], region(zb(k), y))
+        slots[4 + k] = lk.put(region(zb(k), y), region(zb(k), y), ynb)
+
+    def gather_end(slots, region):
+        for k in range(4):
+            lk.got(slots[4 + k], region(zb(k), 1 - y))
+
+    def pk_region(z_, y_):
+        return g.pk.at[:, node(z_, y_)]
+
+    def up_region(z_, y_):
+        return g.w_up_all.at[:, node(z_, y_)]
+
+    def back_region(z_, y_):
+        return g.w_back_all.at[:, y_, :, z_]
+
+    for i, (to, xm, cm, rm) in enumerate(members):
+        lk.got(pk_s[i], g.pk.at[xm, n, cm])
+    pk_g = gather_start(pk_region)
+
+    dn_r = lk.take(4)
+    dn_slot = dn_r + 2 * lax.rem(z, 2) + c
+    dst = g.w_down_all.at[lax.rem(z, 2), y, c]
+    owner = z // 2
+    for k in (1, 2, 3, 0):
+        lk.put_or_keep(
+            g.w_down,
+            dst,
+            lk.take(),
+            dn_slot,
+            dev(x, zo(k), y, owner),
+            jnp.logical_and(owner == c, k == 0),
+        ) if k == 0 else lk.pending.append(
+            (start_of(lk.make(g.w_down, dst, lk.take(), dn_slot, dev(x, zo(k), y, owner))), None)
+        )
+
+    for i, (to, xm, cm, rm) in enumerate(members):
+        lk.got(up_s[i], g.w_up_all.at[xm, n, cm])
+    up_g = gather_start(up_region)
+    for i, (to, xm, cm, rm) in enumerate(members):
+        lk.got(back_s[i], g.w_back_all.at[cm, y, xm, z])
+    back_g = gather_start(back_region)
+
+    for k in (1, 2, 3):
+        gather_pass(pk_g, pk_region, k)
+
+    lk.got(coef_s, g.coef.at[1 - x])
+    cc = g.coef[0].astype(f32)
+    sc = g.coef[1].astype(f32)
+
+    def far(p, _):
+        hr = g.far_re[pl.ds(p, 1), :]
+        hi = g.far_im[pl.ds(p, 1), :]
+        rows = pl.ds(aligned(16 * p, 16), 16)
+        g.state[rows, 0:512] = cc * hr + sc * hi
+        g.state[rows, 512:1024] = sc * hr - cc * hi
+        return 0
+
+    lax.fori_loop(0, 16, far, 0)
+    for half in range(2):
+        rows = slice(128 * half, 128 * half + 128)
+        hi_, lo_ = split(g.state[rows, :])
+        g.kern[rows, :] = (
+            dot(hi_, g.near_hi[...]) + dot(lo_, g.near_hi[...]) + dot(hi_, g.near_lo[...])
+        )
+    ii = lax.broadcasted_iota(jnp.int32, (128, 128), 0)
+    jj = lax.broadcasted_iota(jnp.int32, (128, 128), 1)
+
+    def toeplitz(h, _):
+        prev = jnp.zeros((128, 128), f32)
+        for k in range(16):
+            row = jnp.broadcast_to(g.kern[pl.ds(16 * k + h, 1), :], (128, 128))
+            turned = pltpu.roll(row, 0, 1, stride=1, stride_axis=0)
+            g.toep[h, k] = jnp.where(jj >= ii, turned, prev).astype(bf16)
+            prev = turned
+        return 0
+
+    lax.fori_loop(0, 8, toeplitz, 0)
+    for k in (1, 2, 3):
+        gather_pass(up_g, up_region, k)
+    lax.fori_loop(8, 16, toeplitz, 0)
+
+    gather_end(pk_g, pk_region)
+    e_i = lax.broadcasted_iota(jnp.int32, (128, 1024), 0)
+    e_j = lax.broadcasted_iota(jnp.int32, (128, 1024), 1)
+    spread = jnp.logical_and(e_i < 32, lax.rem(e_j, 32) == e_i).astype(bf16)
+    blk = lax.broadcasted_iota(jnp.int32, (16, 1024), 1) // 32
+    acc = jnp.zeros((16, 1024), f32)
+    for xm in range(2):
+        for nm in range(8):
+            for cm in range(2):
+                rows = g.pk[xm, nm, cm, 32:48, :]
+                acc = acc + jnp.where(
+                    blk == 16 * xm + 2 * nm + cm, dot(rows, spread), 0.0
+                )
+    gain = acc[0:1, :]
+    shift = acc[1:2, :]
+    g.norm_rows[0:1, :] = gain
+    g.norm_rows[1:2, :] = shift
+    wv = g.pk[:, :, :, 0:32, :].reshape(1024, 128)
+    g.w_val[...] = wv
+    g.w_val_t[...] = wv.T
+
+    def norm_block(read, q):
+        def part(s_, _):
+            rows = read(s_).astype(f32)
+            mean = jnp.mean(rows, axis=-1, keepdims=True)
+            cen = rows - mean
+            var = jnp.mean(cen * cen, axis=-1, keepdims=True)
+            out = (cen * lax.rsqrt(var + 1e-5) * g.norm_rows[0:1, :] + g.norm_rows[1:2, :]).astype(
+                bf16
+            )
+            at = aligned(256 * q + 128 * s_, 128)
+            g.normed[pl.ds(at, 128), :] = out
+            g.normed_t[:, pl.ds(at, 128)] = out.T
+            return 0
+
+        lax.fori_loop(0, 2, part, 0)
+        at = pl.ds(aligned(256 * q, 128), 256)
+        pre = dot(g.w_val_t[...], g.normed_t[:, at])
+        act, slope = gelu_parts(pre)
+        g.val_slope[:, at] = slope
+        g.val[:, at] = act.astype(bf16)
+
+    norm_block(lambda s_: g.tokens[s_], r)
+    lk.got(tok_sib, g.tok_all.at[r_sib])
+    norm_block(lambda s_: g.tok_all[r_sib, s_], r_sib)
+    for k in (1, 2, 3):
+        gather_pass(back_g, back_region, k)
+
+    lk.got(tok_x, g.tok_all.at[r_xn])
+    tok_f = lk.put(g.tok_all.at[r_xn], g.tok_all.at[r_xn], sib)
+    norm_block(lambda s_: g.tok_all[r_xn, s_], r_xn)
+    lk.got(tok_f, g.tok_all.at[r_diag])
+    norm_block(lambda s_: g.tok_all[r_diag, s_], r_diag)
+
+    def channel_send(src, landing):
+        slots = []
+        for k in range(1, 8):
+            to = lax.rem(n + k, 8)
+            slots.append(
+                lk.put(
+                    src.at[pl.ds(aligned(16 * to, 16), 16), :],
+                    landing.at[n],
+                    (x, 2 * to + c),
+                )
+            )
+        return slots
+
+    def channel_got(slots, landing):
+        for k in range(1, 8):
+            lk.got(slots[k - 1], landing.at[lax.rem(n + 8 - k, 8)])
+
+    def unpack(landing, out, lead):
+        def one(nm, _):
+            for tb in range(8):
+                s_, cm = 2 * (tb // 4) + tb % 2, (tb // 2) % 2
+                at = aligned(((32 * s_ + lead) + 2 * nm + cm) * 16, 16)
+                out[pl.ds(at, 16), :] = landing[nm, :, 128 * tb : 128 * tb + 128].astype(f32)
+            return 0
+
+        lax.fori_loop(0, 8, one, 0)
+
+    val_s = channel_send(g.val, g.val_in)
+    g.val_in[n] = g.val[pl.ds(aligned(16 * n, 16), 16), :]
+
+    def down_got(zl):
+        for cm in range(2):
+            region = g.w_down_all.at[zl, y, cm]
+            pltpu.make_async_copy(region, region, lk.recv_sems.at[dn_r + 2 * zl + cm]).wait()
+
+    dn_y = []
+    for zl in range(2):
+        down_got(zl)
+        dn_y.append(lk.put(g.w_down_all.at[zl, y], g.w_down_all.at[zl, y], ynb))
+
+    zero = jnp.zeros((256, 128), f32)
+    for s_ in range(4):
+        g.v32[pl.ds(512 * s_, 256), :] = zero
+        g.g32[pl.ds(512 * s_ + 256, 256), :] = zero
+    diag_i = lax.broadcasted_iota(jnp.int32, (32, 32), 0) == lax.broadcasted_iota(
+        jnp.int32, (32, 32), 1
+    )
+    skip_row = jnp.broadcast_to(g.skip[...].astype(f32), (32, 32))
+    g.skip_b[...] = dot(jnp.where(diag_i, skip_row, 0.0).astype(bf16), jnp.ones((32, 128), bf16))
+
+    lk.got(cot_x, g.cot_all.at[r_xn])
+    cot_f = lk.put(g.cot_all.at[r_xn], g.cot_all.at[r_xn], sib)
+
+    channel_got(val_s, g.val_in)
+    unpack(g.val_in, g.v32, 16)
+
+    def conv(h, _):
+        parts = []
+        for k in range(16):
+            rows = [
+                g.v32[pl.ds((32 * s_ + 16 - k) * 16 + h, 16, stride=16), :] for s_ in range(4)
+            ]
+            parts.append(jnp.concatenate(rows, axis=0))
+        out = g.skip_b[pl.ds(16 * x + h, 1), :] * parts[0]
+        for kk in range(8):
+            lhs = jnp.concatenate([parts[2 * kk], parts[2 * kk + 1]], axis=1).astype(bf16)
+            out = out + dot(lhs, g.toep[h, 2 * kk : 2 * kk + 2].reshape(256, 128))
+        g.o32[pl.ds(h, 64, stride=16), :] = out
+        return 0
+
+    def pack(out):
+        def one(nm, _):
+            for tb in range(8):
+                s_, cm = 2 * (tb // 4) + tb % 2, (tb // 2) % 2
+                at = aligned((16 * s_ + 2 * nm + cm) * 16, 16)
+                out[nm, :, 128 * tb : 128 * tb + 128] = g.o32[pl.ds(at, 16), :].astype(bf16)
+            return 0
+
+        lax.fori_loop(0, 8, one, 0)
+
+    def channel_back(src, landing):
+        slots = []
+        for k in range(1, 8):
+            to = lax.rem(n + k, 8)
+            slots.append(
+                lk.put(src.at[to], landing.at[pl.ds(aligned(16 * n, 16), 16), :], (x, 2 * to + c))
+            )
+        return slots
+
+    def channel_back_got(slots, landing):
+        for k in range(1, 8):
+            at = aligned(16 * lax.rem(n + 8 - k, 8), 16)
+            lk.got(slots[k - 1], landing.at[pl.ds(at, 16), :])
+
+    lax.fori_loop(0, 16, conv, 0)
+    pack(g.mix_out)
+    mix_s = channel_back(g.mix_out, g.mix.at[r])
+    g.mix[r, pl.ds(aligned(16 * n, 16), 16), :] = g.mix_out[n]
+
+    gather_end(up_g, up_region)
+
+    def up_tile(i, _):
+        rows = pl.ds(aligned(256 * lax.rem(i, 4), 256), 256)
+        at = pl.ds(aligned(256 * (i // 4), 256), 256)
+        w = g.w_up_all[:, :, :, :, at].reshape(1024, 256)
+        act, slope = gelu_parts(dot(g.normed[rows, :], w))
+        g.act[rows, at] = act
+        g.slope[rows, at] = slope
+        return 0
+
+    lax.fori_loop(0, 12, up_tile, 0)
+    channel_back_got(mix_s, g.mix.at[r])
+    mix_sib = lk.put(g.mix.at[r], g.mix.at[r], sib)
+    mix_x = lk.put(g.mix.at[r], g.mix.at[r], xn)
+    for zl in range(2):
+        lk.got(dn_y[zl], g.w_down_all.at[zl, 1 - y])
+    lk.got(cot_sib, g.cot_all.at[r_sib])
+    lk.got(cot_f, g.cot_all.at[r_diag])
+    down2d = g.w_down_all.reshape(768, 1024)
+
+    def hidden_tile(i, _):
+        q = i // 3
+        at = pl.ds(aligned(256 * lax.rem(i, 3), 256), 256)
+        rows = pl.ds(aligned(256 * q, 256), 256)
+        gh = dot_nt(g.cot_all[q].reshape(256, 1024), down2d[at, :])
+        g.g_gate[rows, at] = (gh * g.act[rows, at]).astype(bf16)
+        g.slope[rows, at] = gh * g.slope[rows, at]
+        return 0
+
+    lax.fori_loop(0, 12, hidden_tile, 0)
+    lk.got(mix_x, g.mix.at[r_xn])
+    mix_f = lk.put(g.mix.at[r_xn], g.mix.at[r_xn], sib)
+    gather_end(back_g, back_region)
+    back2d = g.w_back_all.reshape(512, 768)
+
+    def mixed_part(xm, cm, q):
+        w = back2d[pl.ds(aligned(128 * (2 * xm + cm), 128), 128), :]
+        return dot_nt(w, g.g_gate[pl.ds(aligned(256 * q, 256), 256), :])
+
+    def gm_sib(i, _):
+        xm, q = i // 4, lax.rem(i, 4)
+        at = pl.ds(aligned(256 * q, 128), 256)
+        g.gm_send[xm, :, at] = mixed_part(xm, 1 - c, q).astype(bf16)
+        return 0
+
+    lax.fori_loop(0, 8, gm_sib, 0)
+    gm_s = lk.put(g.gm_send, g.gm_in, sib)
+
+    def gm_far_add(q, _):
+        at = pl.ds(aligned(256 * q, 128), 256)
+        g.gm_x[:, at] = (mixed_part(1 - x, c, q) + g.gm_in[1 - x, :, at].astype(f32)).astype(bf16)
+        return 0
+
+    lk.got(gm_s, g.gm_in)
+    lax.fori_loop(0, 4, gm_far_add, 0)
+    gm_xs = lk.put(g.gm_x, g.gm_xin, xn)
+
+    lk.got(mix_sib, g.mix.at[r_sib])
+    lk.got(mix_f, g.mix.at[r_diag])
+
+    def turn(i, _):
+        rr, tb = i // 8, lax.rem(i, 8)
+        rows = pl.ds(aligned(128 * tb, 128), 128)
+        at = pl.ds(aligned(128 * rr, 128), 128)
+        g.mix_tok[rows, at] = g.mix[rr, :, rows].T
+        return 0
+
+    lax.fori_loop(0, 32, turn, 0)
+
+    def gate_tile(i, _):
+        q = i // 3
+        rows = pl.ds(aligned(256 * q, 256), 256)
+        at = pl.ds(aligned(256 * lax.rem(i, 3), 256), 256)
+        gate = dot(g.mix_tok[rows, :], back2d[:, at])
+        hidden = (g.act[rows, at] * gate).astype(bf16)
+        g.hidden[rows, at] = hidden
+        g.hidden_t[at, rows] = hidden.T
+        g.g_up[rows, at] = (g.slope[rows, at] * gate).astype(bf16)
+        return 0
+
+    lax.fori_loop(0, 12, gate_tile, 0)
+
+    def gm_own(q, _):
+        at = pl.ds(aligned(256 * q, 128), 256)
+        g.gm[:, at] = (
+            mixed_part(x, c, q) + g.gm_in[x, :, at].astype(f32) + g.gm_xin[:, at].astype(f32)
+        ).astype(bf16)
+        return 0
+
+    lk.got(gm_xs, g.gm_xin)
+    lax.fori_loop(0, 4, gm_own, 0)
+    gm_cs = channel_send(g.gm, g.gm_land)
+    g.gm_land[n] = g.gm[pl.ds(aligned(16 * n, 16), 16), :]
+
+    cot2d = g.cot_all.reshape(1024, 1024)
+    gd_y = []
+    for zl in range(2):
+
+        def down_tile(i, _):
+            rows = pl.ds(aligned(384 * zl + 192 * (i // 4), 64), 192)
+            at = pl.ds(aligned(256 * lax.rem(i, 4), 256), 256)
+            g.gd[zl, i // 4, :, at] = dot(g.hidden_t[rows, :], cot2d[:, at]).astype(bf16)
+            return 0
+
+        lax.fori_loop(0, 8, down_tile, 0)
+        gd_y.append(lk.put(g.gd.at[zl, 1 - y], g.gd_y.at[zl], ynb))
+
+    up_y = []
+
+    def up_grad(k):
+        z_d = zo(k)
+        for xm in range(2):
+            t = 4 * xm + z_d
+
+            def tile(i, _):
+                rows = pl.ds(aligned(128 * t, 128), 128)
+                at = pl.ds(aligned(256 * i, 256), 256)
+                g.gu[xm, z_d, :, at] = dot(g.normed_t[rows, :], g.g_up[:, at]).astype(bf16)
+                return 0
+
+            lax.fori_loop(0, 3, tile, 0)
+            other = pl.ds(aligned(64 * (1 - y), 64), 64)
+            up_y.append((t, lk.put(g.gu.at[xm, z_d, other], g.gu_y.at[t], ynb)))
+
+    own64 = pl.ds(aligned(64 * y, 64), 64)
+    gu_s = {}
+
+    def up_sum(i, k):
+        z_d = zo(k)
+        for xm in range(2):
+            t, slot = up_y[2 * i + xm]
+            lk.got(slot, g.gu_y.at[t])
+            total = g.gu[xm, z_d, own64, :].astype(f32) + g.gu_y[t].astype(f32)
+            g.gu[xm, z_d, own64, :] = total.astype(bf16)
+        if k:
+            gu_s[k] = lk.put(g.gu.at[:, z_d, own64], g.gu_in.at[k - 1], dev(x, z_d, y, c))
+
+    gd_r = lk.take(4)
+
+    def down_sum(zl):
+        lk.got(gd_y[zl], g.gd_y.at[zl])
+        for cm in range(2):
+            part = pl.ds(96 * cm, 96)
+            total = g.gd[zl, y, part, :].astype(f32) + g.gd_y[zl, part, :].astype(f32)
+            g.gd[zl, y, part, :] = total.astype(bf16)
+            z_d = 2 * c + zl
+            here = jnp.logical_and(z_d == z, c == cm)
+            lk.put_or_keep(
+                g.gd.at[zl, y, part], g.gd_in.at[z], lk.take(), gd_r + z, dev(x, z_d, y, cm), here
+            )
+
+    up_grad(1)
+    down_sum(0)
+    up_grad(2)
+    down_sum(1)
+    up_sum(0, 1)
+    up_grad(3)
+    up_sum(1, 2)
+    up_grad(0)
+    up_sum(2, 3)
+
+    mix2d = g.mix.reshape(512, 1024)
+
+    def back_tile(rr):
+        def tile(i, _):
+            at = pl.ds(aligned(256 * i, 256), 256)
+            rows = pl.ds(aligned(128 * rr, 128), 128)
+            g.gb[rr // 2, lax.rem(rr, 2), :, at] = dot(
+                mix2d[rows, :], g.g_gate[:, at]
+            ).astype(bf16)
+            return 0
+
+        lax.fori_loop(0, 3, tile, 0)
+
+    gb_y = []
+    for cm in range(2):
+        back_tile(2 * cm + 1 - y)
+        gb_y.append(lk.put(g.gb.at[cm, 1 - y], g.gb_y.at[cm], ynb))
+    up_sum(3, 0)
+    for cm in range(2):
+        back_tile(2 * cm + y)
+
+    channel_got(gm_cs, g.gm_land)
+    unpack(g.gm_land, g.g32, 0)
+    g.xs[:, 2048:2176] = jnp.zeros((128, 128), f32)
+
+    def conv_back(h, _):
+        parts = []
+        for k in range(16):
+            rows = [g.g32[pl.ds((32 * s_ + k) * 16 + h, 16, stride=16), :] for s_ in range(4)]
+            parts.append(jnp.concatenate(rows, axis=0))
+        own = [g.v32[pl.ds((32 * s_ + 16) * 16 + h, 16, stride=16), :] for s_ in range(4)]
+        own = jnp.concatenate(own, axis=0)
+        g.skip_part[pl.ds(h, 1), :] = jnp.sum(own * parts[0], axis=0, keepdims=True)
+        own_t = own.T.astype(bf16)
+        out = g.skip_b[pl.ds(16 * x + h, 1), :] * parts[0]
+        for kk in range(8):
+            lhs = jnp.concatenate([parts[2 * kk], parts[2 * kk + 1]], axis=1).astype(bf16)
+            rhs = jnp.concatenate([g.toep[h, 2 * kk], g.toep[h, 2 * kk + 1]], axis=1)
+            out = out + dot_nt(lhs, rhs)
+            g.xs[:, 256 * kk : 256 * kk + 256] = dot(own_t, lhs)
+        g.o32[pl.ds(h, 64, stride=16), :] = out
+
+        acc = g.xs[120:128, :]
+        for b in range(14, -1, -1):
+            acc = pltpu.roll(acc, 2176 - 8, 1) + g.xs[8 * b : 8 * b + 8, :]
+        for k in range(17):
+            at = pl.ds(aligned(128 * k + 8 * h, 8), 8)
+            g.gk8[at, :] = acc[:, 128 * k : 128 * k + 128]
+        return 0
+
+    lax.fori_loop(0, 16, conv_back, 0)
+    pack(g.gv_out)
+    gv_s = channel_back(g.gv_out, g.g_val)
+    g.g_val[pl.ds(aligned(16 * n, 16), 16), :] = g.gv_out[n]
+
+    for cm in range(2):
+        lk.got(gb_y[cm], g.gb_y.at[cm])
+        total = g.gb[cm, y].astype(f32) + g.gb_y[cm].astype(f32)
+        g.gb_z[pl.ds(2 * cm, 2)] = total.astype(bf16).reshape(2, 4, 16, 768)
+    gb_s = {}
+    for k in (1, 2, 3):
+        gb_s[k] = lk.put(g.gb_z.at[:, zo(k)], g.gb_in.at[k - 1], dev(x, zo(k), y, c))
+
+
+    def gk_rows(s_):
+        tiles = [g.gk8[pl.ds(128 * k + s_, 16, stride=8), :] for k in range(17)]
+        return jnp.concatenate(tiles, axis=1)
+
+    acc = gk_rows(7)
+    for s_ in range(6, -1, -1):
+        acc = pltpu.roll(acc, 2176 - 1, 1) + gk_rows(s_)
+    g.gk[...] = acc
+    for half in range(2):
+        tall = jnp.concatenate(
+            [g.gk[:, 128 * k : 128 * k + 128] for k in range(8 * half, 8 * half + 8)], axis=0
+        )
+        hi_, lo_ = split(tall)
+        g.state[128 * half : 128 * half + 128, :] = (
+            dot(hi_, g.near_t_hi[...]) + dot(lo_, g.near_t_hi[...]) + dot(hi_, g.near_t_lo[...])
+        )
+
+    def far_back(p, carry):
+        gc, gs = carry
+        hr = g.far_re[pl.ds(p, 1), :]
+        hi = g.far_im[pl.ds(p, 1), :]
+        rows = pl.ds(aligned(16 * p, 16), 16)
+        ur = g.state[rows, 0:512]
+        ui = g.state[rows, 512:1024]
+        return gc + hr * ur - hi * ui, gs + hr * ui + hi * ur
+
+    blank = jnp.zeros((16, 512), f32)
+    gc, gs = lax.fori_loop(0, 16, far_back, (blank, blank))
+    g.gcoef[0] = gc
+    g.gcoef[1] = gs
+    gcoef_s = lk.put(g.gcoef.at[1 - x], g.gcoef_in, xn)
+    g.skip_sum[...] = jnp.broadcast_to(jnp.sum(g.skip_part[...], axis=1, keepdims=True), (16, 128))
+    skip_s = lk.put(g.skip_sum, g.skip_in, xn)
+
+    def group_sum(part, send, land, xsend, xland):
+        def to_sib(i, _):
+            xm, j = i // 4, lax.rem(i, 4)
+            at = pl.ds(aligned(256 * j, 256), 256)
+            send[xm, :, at] = part(xm, 1 - c, at).astype(bf16)
+            return 0
+
+        lax.fori_loop(0, 8, to_sib, 0)
+        first = lk.put(send, land, sib)
+
+        def add_far(j, _):
+            at = pl.ds(aligned(256 * j, 256), 256)
+            xsend[:, at] = (part(1 - x, c, at) + land[1 - x, :, at].astype(f32)).astype(bf16)
+            return 0
+
+        lk.got(first, land)
+        lax.fori_loop(0, 4, add_far, 0)
+        second = lk.put(xsend, xland, xn)
+
+        def own(at):
+            return part(x, c, at) + land[x, :, at].astype(f32) + xland[:, at].astype(f32)
+
+        return second, own
+
+    spare = g.normed.reshape(2, 2, 256, 1024)
+
+    def branch_part(xm, cm, at):
+        rows = pl.ds(aligned(256 * (2 * xm + cm), 256), 256)
+        return dot(g.hidden[rows, :], down2d[:, at])
+
+    br_s, br_own = group_sum(
+        branch_part, spare.at[0], g.br_in, g.tok_all.at[r].reshape(256, 1024), g.br_xin
+    )
+
+    channel_back_got(gv_s, g.g_val)
+    gvp = (g.g_val[...].astype(f32) * g.val_slope[...]).astype(bf16)
+    g.gvp_t[...] = gvp.T
+
+    def val_tile(t, _):
+        rows = pl.ds(aligned(128 * t, 128), 128)
+        g.gv[t] = dot(g.normed_t[rows, :], g.gvp_t[...]).astype(bf16)
+        return 0
+
+    lax.fori_loop(0, 8, val_tile, 0)
+    other = pl.ds(aligned(64 * (1 - y), 64), 64)
+    gv_y = lk.put(g.gv.at[:, other], g.gv_y, ynb)
+
+    up2d = g.w_up_all.reshape(1024, 768)
+
+    def normed_part(xm, cm, at):
+        rows = pl.ds(aligned(256 * (2 * xm + cm), 256), 256)
+        return dot_nt(g.g_up[rows, :], up2d[at, :]) + dot_nt(g.gvp_t[rows, :], g.w_val[at, :])
+
+    gn_s, gn_own = group_sum(
+        normed_part, spare.at[1], g.gn_in, g.tok_all.at[r_sib].reshape(256, 1024), g.gn_xin
+    )
+
+    lk.got(gv_y, g.gv_y)
+    total = (g.gv[:, own64, :].astype(f32) + g.gv_y[...].astype(f32)).astype(bf16)
+    g.gv_z[...] = total.reshape(2, 4, 64, 128)
+    gv_zs = {}
+    for k in (1, 2, 3):
+        gv_zs[k] = lk.put(g.gv_z.at[:, zo(k)], g.gv_in.at[k - 1], dev(x, zo(k), y, c))
+
+    for k in (1, 2, 3):
+        lk.got(gu_s[k], g.gu_in.at[k - 1])
+    total = g.gu[:, z, own64, :].astype(f32)
+    for k in range(3):
+        total = total + g.gu_in[k].astype(f32)
+    g.gu_f[...] = total.reshape(2, 2, 32, 768).astype(bf16)
+    for k in (1, 2, 3):
+        lk.got(gb_s[k], g.gb_in.at[k - 1])
+    total = g.gb_z[:, z].astype(f32)
+    for k in range(3):
+        total = total + g.gb_in[k].astype(f32)
+    g.gb_f[...] = total.astype(bf16)
+    fin_u = [lk.put(g.gu_f.at[xm, cm], g.fu_in.at[r], to) for to, xm, cm, rm in members]
+    fin_b = [lk.put(g.gb_f.at[2 * cm + xm], g.fb_in.at[r], to) for to, xm, cm, rm in members]
+    g.fu_in[r] = g.gu_f[x, c]
+    g.fb_in[r] = g.gb_f[2 * c + x]
+
+    lk.got(br_s, g.br_xin)
+
+    def result_tile(j, _):
+        at = pl.ds(aligned(256 * j, 256), 256)
+        out = br_own(at).reshape(2, 128, 256) + g.tokens[:, :, at].astype(f32)
+        g.result[:, :, at] = out.astype(bf16)
+        return 0
+
+    lax.fori_loop(0, 4, result_tile, 0)
+
+    for zs in range(4):
+        region = g.gd_in.at[zs]
+        pltpu.make_async_copy(region, region, lk.recv_sems.at[gd_r + zs]).wait()
+    total = g.gd_in[0].astype(f32)
+    for zs in range(1, 4):
+        total = total + g.gd_in[zs].astype(f32)
+    g.o_down[...] = total
+
+    for k in (1, 2, 3):
+        lk.got(gv_zs[k], g.gv_in.at[k - 1])
+    total = g.gv_z[:, z].astype(f32)
+    for k in range(3):
+        total = total + g.gv_in[k].astype(f32)
+    g.gv_f[...] = total.reshape(2, 2, 32, 128).astype(bf16)
+    fin_v = [lk.put(g.gv_f.at[xm, cm], g.fv_in.at[r], to) for to, xm, cm, rm in members]
+    g.fv_in[r] = g.gv_f[x, c]
+
+    mine = pl.ds(aligned(16 * x, 16), 16)
+    theirs = pl.ds(aligned(16 * (1 - x), 16), 16)
+    lk.got(gcoef_s, g.gcoef_in)
+    g.o_coef[mine, :] = g.gcoef[x]
+    g.o_coef[theirs, :] = g.gcoef_in[...]
+    lk.got(skip_s, g.skip_in)
+    g.o_skip[mine, :] = g.skip_sum[...]
+    g.o_skip[theirs, :] = g.skip_in[...]
+
+    for i, (to, xm, cm, rm) in enumerate(members):
+        lk.got(fin_u[i], g.fu_in.at[rm])
+        lk.got(fin_b[i], g.fb_in.at[rm])
+    for rr in range(4):
+        g.o_up[:, 768 * rr : 768 * rr + 768] = g.fu_in[rr].astype(f32)
+        g.o_back[:, 768 * rr : 768 * rr + 768] = g.fb_in[rr].astype(f32)
+
+    lk.got(gn_s, g.gn_xin)
+
+    def gn_tile(j, _):
+        at = pl.ds(aligned(256 * j, 256), 256)
+        g.state[:, at] = gn_own(at)
+        return 0
+
+    lax.fori_loop(0, 4, gn_tile, 0)
+
+    def norm_back(i, carry):
+        dg, ds = carry
+        s_, part = i // 2, pl.ds(aligned(64 * lax.rem(i, 2), 64), 64)
+        rows = g.tokens[s_, part, :].astype(f32)
+        mean = jnp.mean(rows, axis=-1, keepdims=True)
+        cen = rows - mean
+        var = jnp.mean(cen * cen, axis=-1, keepdims=True)
+        inv = lax.rsqrt(var + 1e-5)
+        zn = cen * inv
+        gn = g.state[pl.ds(aligned(64 * i, 64), 64), :]
+        gg = gn * g.norm_rows[0:1, :]
+        m1 = jnp.mean(gg, axis=-1, keepdims=True)
+        m2 = jnp.mean(gg * zn, axis=-1, keepdims=True)
+        g.g_tokens[s_, part, :] = g.cot[s_, part, :].astype(f32) + inv * (gg - m1 - zn * m2)
+        dg = dg + jnp.sum(gn * zn, axis=0, keepdims=True)
+        ds = ds + jnp.sum(gn, axis=0, keepdims=True)
+        return dg, ds
+
+    blank = jnp.zeros((1, 1024), f32)
+    dg, ds = lax.fori_loop(0, 4, norm_back, (blank, blank))
+    for zd in range(4):
+        g.ng[zd, 0:1, :] = dg[:, 128 * zd : 128 * zd + 128]
+        g.ng[zd, 1:2, :] = dg[:, 512 + 128 * zd : 640 + 128 * zd]
+        g.ng[zd, 2:3, :] = ds[:, 128 * zd : 128 * zd + 128]
+        g.ng[zd, 3:4, :] = ds[:, 512 + 128 * zd : 640 + 128 * zd]
+        g.ng[zd, 4:8, :] = jnp.zeros((4, 128), f32)
+    ng_s = []
+    for k in range(1, 8):
+        to = lax.rem(n + k, 8)
+        ng_s.append(lk.put(g.ng.at[to // 2], g.ng_in.at[k - 1], (x, 2 * to + c)))
+    for i, (to, xm, cm, rm) in enumerate(members):
+        lk.got(fin_v[i], g.fv_in.at[rm])
+    wide = jnp.concatenate([g.fv_in[rr] for rr in range(4)], axis=1)
+    g.o_value[...] = dot_nt(wide, g.perm[...])
+    total = g.ng[z]
+    for k in range(1, 8):
+        lk.got(ng_s[k - 1], g.ng_in.at[k - 1])
+        total = total + g.ng_in[k - 1]
+    g.ng_f[...] = total
+    ng_t = [lk.put(g.ng_f, g.ng_fin.at[i], to) for i, (to, xm, cm, rm) in enumerate(members)]
+    for i in range(3):
+        lk.got(ng_t[i], g.ng_fin.at[i])
+        total = total + g.ng_fin[i]
+    total = jnp.where(x == 0, total, pltpu.roll(total, 7, 0))
+    g.o_norm[...] = pltpu.roll(total, 128 - (64 * y + 32 * c), 1)
+    lk.finish()
+    assert lk.count <= N_SEMS
+
+
+def start_of(copy):
+    copy.start()
+    return copy
+
+
+def fast_body(
+    tokens, norm_gain, norm_shift, w_up, w_value, w_back, w_down, mode_coef, skip_gain, cotangent
+):
+    states = 512
+    length = tokens.shape[1] * lax.axis_size("tok")
+    far_re, far_im, near_hi, near_lo, near_t_hi, near_t_lo = mode_tables(states, length)
+    ins = dict(
+        tokens=tokens,
+        norm_gain=norm_gain.reshape(1, -1),
+        norm_shift=norm_shift.reshape(1, -1),
+        w_up=w_up,
+        w_value=w_value,
+        w_back=w_back,
+        w_down=w_down,
+        mode_coef=mode_coef,
+        skip=skip_gain.reshape(1, -1),
+        cot=cotangent,
+        far_re=far_re,
+        far_im=far_im,
+        near_hi=near_hi,
+        near_lo=near_lo,
+        near_t_hi=near_t_hi,
+        near_t_lo=near_t_lo,
+    )
+    outs = dict(
+        result=((2, 128, 1024), bf16),
+        g_tokens=((2, 128, 1024), f32),
+        o_norm=((8, 128), f32),
+        o_up=((32, 3072), f32),
+        o_value=((32, 512), f32),
+        o_back=((16, 3072), f32),
+        o_down=((96, 1024), f32),
+        o_coef=((32, 512), f32),
+        o_skip=((32, 128), f32),
+    )
+    scratch = dict(
+        perm=((512, 512), bf16),
+        pk_send=((4, 48, 128), bf16),
+        pk=((2, 8, 2, 48, 128), bf16),
+        coef=((2, 16, 512), bf16),
+        w_up_all=((2, 8, 2, 32, 768), bf16),
+        w_back_all=((2, 2, 2, 4, 16, 768), bf16),
+        w_down_all=((2, 2, 2, 96, 1024), bf16),
+        tok_all=((4, 2, 128, 1024), bf16),
+        cot_all=((4, 2, 128, 1024), bf16),
+        state=((256, 1024), f32),
+        kern=((256, 128), f32),
+        toep=((16, 16, 128, 128), bf16),
+        norm_rows=((8, 1024), f32),
+        w_val=((1024, 128), bf16),
+        w_val_t=((128, 1024), bf16),
+        normed=((1024, 1024), bf16),
+        normed_t=((1024, 1024), bf16),
+        val_slope=((128, 1024), f32),
+        val=((128, 1024), bf16),
+        val_in=((8, 16, 1024), bf16),
+        v32=((2048, 128), f32),
+        g32=((2048, 128), f32),
+        o32=((1024, 128), f32),
+        skip_b=((32, 128), f32),
+        mix_out=((8, 16, 1024), bf16),
+        mix=((4, 128, 1024), bf16),
+        act=((1024, 768), f32),
+        slope=((1024, 768), f32),
+        g_gate=((1024, 768), bf16),
+        gm_send=((2, 128, 1024), bf16),
+        gm_in=((2, 128, 1024), bf16),
+        gm_x=((128, 1024), bf16),
+        gm_xin=((128, 1024), bf16),
+        gm=((128, 1024), bf16),
+        gm_land=((8, 16, 1024), bf16),
+        mix_tok=((1024, 512), bf16),
+        hidden=((1024, 768), bf16),
+        hidden_t=((768, 1024), bf16),
+        g_up=((1024, 768), bf16),
+        gd=((2, 2, 192, 1024), bf16),
+        gd_y=((2, 192, 1024), bf16),
+        gd_in=((4, 96, 1024), bf16),
+        gu=((2, 4, 128, 768), bf16),
+        gu_y=((8, 64, 768), bf16),
+        gu_in=((3, 2, 64, 768), bf16),
+        gu_f=((2, 2, 32, 768), bf16),
+        fu_in=((4, 32, 768), bf16),
+        gb=((2, 2, 128, 768), bf16),
+        gb_y=((2, 128, 768), bf16),
+        gb_z=((4, 4, 16, 768), bf16),
+        gb_in=((3, 4, 16, 768), bf16),
+        gb_f=((4, 16, 768), bf16),
+        fb_in=((4, 16, 768), bf16),
+        gv=((8, 128, 128), bf16),
+        gv_y=((8, 64, 128), bf16),
+        gv_z=((2, 4, 64, 128), bf16),
+        gv_in=((3, 2, 64, 128), bf16),
+        gv_f=((2, 2, 32, 128), bf16),
+        fv_in=((4, 32, 128), bf16),
+        xs=((128, 2176), f32),
+        gk8=((2176, 128), f32),
+        gk=((16, 2176), f32),
+        skip_part=((16, 128), f32),
+        skip_sum=((16, 128), f32),
+        skip_in=((16, 128), f32),
+        gcoef=((2, 16, 512), f32),
+        gcoef_in=((16, 512), f32),
+        gv_out=((8, 16, 1024), bf16),
+        g_val=((128, 1024), bf16),
+        gvp_t=((1024, 128), bf16),
+        br_in=((2, 256, 1024), bf16),
+        br_xin=((256, 1024), bf16),
+        gn_in=((2, 256, 1024), bf16),
+        gn_xin=((256, 1024), bf16),
+        ng=((4, 8, 128), f32),
+        ng_in=((7, 8, 128), f32),
+        ng_f=((8, 128), f32),
+        ng_fin=((3, 8, 128), f32),
+    )
+    names = list(ins) + list(outs) + list(scratch) + ["ssem", "rsem"]
+    vmem = pl.BlockSpec(memory_space=pltpu.VMEM)
+    got = pl.pallas_call(
+        functools.partial(layer_kernel, names),
+        out_shape=[jax.ShapeDtypeStruct(s, t) for s, t in outs.values()],
+        in_specs=[vmem] * len(ins),
+        out_specs=[vmem] * len(outs),
+        scratch_shapes=[pltpu.VMEM(s, t) for s, t in scratch.values()]
+        + [pltpu.SemaphoreType.DMA((N_SEMS,)), pltpu.SemaphoreType.DMA((N_SEMS,))],
+        compiler_params=pltpu.CompilerParams(
+            collective_id=0, has_side_effects=True, vmem_limit_bytes=64 << 20
+        ),
+    )(*ins.values())
+    o = types.SimpleNamespace(**dict(zip(outs, got)))
+    return (
+        o.result,
+        o.g_tokens,
+        o.o_norm[0, :32],
+        o.o_norm[2, :32],
+        o.o_up,
+        o.o_value,
+        o.o_back,
+        o.o_down,
+        o.o_coef,
+        o.o_skip[:, 0],
+    )
+
+
+def run(tokens, *rest):
+    sizes = (lax.axis_size("item"), lax.axis_size("tok"), tokens.shape)
+    if sizes == (2, 16, (2, 128, 1024)):
+        return fast_body(tokens, *rest)
+    return body(tokens, *rest)
+
+
 def solution(mesh):
     in_specs = (
         P("item", "tok", None),
@@ -246,4 +1272,4 @@
         P("tok", "item"),
         P("tok"),
     )
-    return jax.shard_map(body, mesh=mesh, in_specs=in_specs, out_specs=out_specs, check_vma=False)
+    return jax.shard_map(run, mesh=mesh, in_specs=in_specs, out_specs=out_specs, check_vma=False)

time: 914 us -> 237 us (0.26)
  waiting for transfers between devices: 547 us -> 0 us
  Pallas kernels: 0 us -> 227 us
  matrix products: 115 us -> 0 us
  blocking collectives: 109 us -> 0 us
  local copies, waits for them, and re-layouts: 75.2 us -> 9.46 us
  other arithmetic: 27.5 us -> 0 us
  starting transfers between devices: 16.2 us -> 0 us
  between operations: 15.2 us -> 0.67 us
    unnamed x7 -> x0, waiting for transfers between devices: 427 us -> none
    pallas_call x0 -> x1, Pallas kernels: none -> 227 us  [fast_body(): pl.pallas_call(functools.partial(layer_kernel, names), out_shape=[jax.Sha...]
    dot_general x50 -> x0, matrix products: 115 us -> none  [the longest x24 32.1 us: right_product(): return jnp.einsum('...kq,qm->...km', left_part, table, precision=highest)]
    all_gather x4 -> x0, waiting for transfers between devices: 108 us -> none  [the longest x1 64.3 us: body(): lax.all_gather(w_down, ('item', 'tok'), axis=0, tiled=True)]
    unnamed x2 -> x0, blocking collectives: 84.3 us -> none
    reshape x10 -> x0, local copies, waits for them, and re-layouts: 31.2 us -> none  [the longest x1 10 us: body(): up_flat = grad_w_up.reshape(owners, -1)]
    unnamed x61 -> x19, local copies, waits for them, and re-layouts: 25.5 us -> 6.77 us
    mul x1 -> x0, other arithmetic: 17.5 us -> none  [basis_block(): decays * jnp.cos(phase_turns)]
  transfers between devices with their start and end apart: 9 -> 0, of which waited for: 5 -> 0; matrix products, arithmetic and copies ran while one was open for 18% -> 0% of each run, Pallas kernels for 0% -> 0%
where the time goes in v1:
time: 237 us
  Pallas kernels  227 us (96%)
  local copies, waits for them, and re-layouts  9.46 us (4%)
    pallas_call x1, Pallas kernels, fast_body(): pl.pallas_call(functools.partial(layer_kernel, names), out_shape=[jax.Sha...  227 us
    unnamed x19, local copies, waits for them, and re-layouts  6.77 us

profile of v1, /device:TPU:0, one launch (start us, length us, event | category | flops | bytes accessed | tf_op | source)
XLA Modules:
  0.0 236.7 jit_solution(10418168342477745865)
XLA Ops:
  0.6 226.6 %shard_map.231 = (bf16[2,128,1024]{2,1,0:T(8,128)(2,1)}, f32[2,128,1024]{2,1,0:T(8,128)}, f32[8,128]{1,0:T(8,128)}, f32[32,3072]{1,0:T(8,128)}, f32[32,512]{1,0:...) custom-call(bf16[2,128,1024]{2,1,0:T(8,128)(2,1)} %refs_0_.1, ...), custom_call_target="tpu_custom_call" | custom-call | tf_op jit(solution)/shard_map/pallas_call | solution.py:1217
  227.2 0.0 copy-start
  227.2 1.4 slice_reduce_fusion
  228.7 1.3 slice_bitcast_fusion
  229.9 1.9 copy.33
  231.8 0.0 copy-done
  231.8 0.0 copy-start.2
  231.8 1.0 copy.34
  232.8 0.3 copy-done.2
  233.0 0.0 copy-start.5
  233.0 0.0 copy-start.3
  233.1 0.7 copy.35
  233.8 0.1 copy-done.5
  233.9 0.0 copy-start.1
  233.9 0.6 copy.36
  234.5 0.0 copy-done.3
  234.5 0.7 copy.37
  235.2 0.0 copy-done.1
  235.2 0.0 copy-start.4
  235.2 0.7 copy.38
  236.0 0.1 copy-done.4
  236.1 0.6 copy.39
Async XLA Ops:
  227.2 4.6 %copy-start = (f32[2,128,1024]{2,1,0:T(8,128)S(1)}, f32[2,128,1024]{2,1,0:T(8,128)}, u32[]{:S(2)}) copy-start(f32[2,128,1024]{2,1,0:T(8,128)} %get-tuple-element.41) | copy-start | bytes 3145732
  231.8 1.2 copy-start.2
  233.0 0.9 copy-start.5
  233.0 1.5 copy-start.3
  233.9 1.3 copy-start.1
  235.2 0.9 copy-start.4

commit v2 on v1

--- a/solution.py
+++ b/solution.py
@@ -271,8 +271,8 @@
         far_im.T.astype(np.float32).copy(),
         high,
         low,
-        high.T.copy(),
-        low.T.copy(),
+        high.T[::-1].copy(),
+        low.T[::-1].copy(),
     )
 
 
@@ -388,6 +388,7 @@
     for to, xm, cm, rm in members:
         pk_s.append(lk.put(g.pk_send.at[rm], g.pk.at[x, n, c], to))
     coef_s = lk.put(g.mode_coef.at[pl.ds(aligned(16 * (1 - x), 16), 16), :], g.coef.at[x], xn)
+    tok_x = lk.put(g.tokens, g.tok_all.at[r], xn)
     my_back = g.w_back_all.at[c, y, x, z]
 
     def cols(rm):
@@ -398,9 +399,8 @@
     for to, xm, cm, rm in members:
         back_s.append(lk.put(g.w_back.at[:, cols(rm)], my_back, to))
     tok_sib = lk.put(g.tokens, g.tok_all.at[r], sib)
-    tok_x = lk.put(g.tokens, g.tok_all.at[r], xn)
+    cot_x = lk.put(g.cot, g.cot_all.at[r], xn)
     cot_sib = lk.put(g.cot, g.cot_all.at[r], sib)
-    cot_x = lk.put(g.cot, g.cot_all.at[r], xn)
     g.pk[x, n, c] = g.pk_send[r]
     g.w_up_all[x, n, c] = g.w_up[:, cols(r)]
     g.w_back_all[c, y, x, z] = g.w_back[:, cols(r)]
@@ -439,27 +439,20 @@
     dn_slot = dn_r + 2 * lax.rem(z, 2) + c
     dst = g.w_down_all.at[lax.rem(z, 2), y, c]
     owner = z // 2
-    for k in (1, 2, 3, 0):
-        lk.put_or_keep(
-            g.w_down,
-            dst,
-            lk.take(),
-            dn_slot,
-            dev(x, zo(k), y, owner),
-            jnp.logical_and(owner == c, k == 0),
-        ) if k == 0 else lk.pending.append(
+    lk.put_or_keep(g.w_down, dst, lk.take(), dn_slot, dev(x, z, y, owner), owner == c)
+    for k in (1, 2, 3):
+        lk.pending.append(
             (start_of(lk.make(g.w_down, dst, lk.take(), dn_slot, dev(x, zo(k), y, owner))), None)
         )
-
-    for i, (to, xm, cm, rm) in enumerate(members):
-        lk.got(up_s[i], g.w_up_all.at[xm, n, cm])
-    up_g = gather_start(up_region)
-    for i, (to, xm, cm, rm) in enumerate(members):
-        lk.got(back_s[i], g.w_back_all.at[cm, y, xm, z])
-    back_g = gather_start(back_region)
-
-    for k in (1, 2, 3):
-        gather_pass(pk_g, pk_region, k)
+    dn_first = jnp.where(owner == c, lax.rem(z, 2), 1 - c)
+    dn_y = lk.take(2)
+
+    def down_pass(zl):
+        for cm in range(2):
+            region = g.w_down_all.at[zl, y, cm]
+            pltpu.make_async_copy(region, region, lk.recv_sems.at[dn_r + 2 * zl + cm]).wait()
+        region = g.w_down_all.at[zl, y]
+        lk.pending.append((start_of(lk.make(region, region, lk.take(), dn_y + zl, ynb)), None))
 
     lk.got(coef_s, g.coef.at[1 - x])
     cc = g.coef[0].astype(f32)
@@ -480,8 +473,11 @@
         g.kern[rows, :] = (
             dot(hi_, g.near_hi[...]) + dot(lo_, g.near_hi[...]) + dot(hi_, g.near_lo[...])
         )
+    for k in (1, 2, 3):
+        gather_pass(pk_g, pk_region, k)
     ii = lax.broadcasted_iota(jnp.int32, (128, 128), 0)
     jj = lax.broadcasted_iota(jnp.int32, (128, 128), 1)
+    flip = (ii + jj == 127).astype(bf16)
 
     def toeplitz(h, _):
         prev = jnp.zeros((128, 128), f32)
@@ -492,10 +488,8 @@
             prev = turned
         return 0
 
-    lax.fori_loop(0, 8, toeplitz, 0)
-    for k in (1, 2, 3):
-        gather_pass(up_g, up_region, k)
-    lax.fori_loop(8, 16, toeplitz, 0)
+    lax.fori_loop(0, 16, toeplitz, 0)
+    down_pass(dn_first)
 
     gather_end(pk_g, pk_region)
     e_i = lax.broadcasted_iota(jnp.int32, (128, 1024), 0)
@@ -516,7 +510,10 @@
     g.norm_rows[1:2, :] = shift
     wv = g.pk[:, :, :, 0:32, :].reshape(1024, 128)
     g.w_val[...] = wv
-    g.w_val_t[...] = wv.T
+    wvt = wv.T
+    for t in range(8):
+        at = 256 * (t % 4) + 128 * (t // 4)
+        g.w_val_t[:, at : at + 128] = wvt[:, 128 * t : 128 * t + 128]
 
     def norm_block(read, q):
         def part(s_, _):
@@ -529,7 +526,9 @@
             )
             at = aligned(256 * q + 128 * s_, 128)
             g.normed[pl.ds(at, 128), :] = out
-            g.normed_t[:, pl.ds(at, 128)] = out.T
+            for t in range(8):
+                low = 256 * (t % 4) + 128 * (t // 4)
+                g.normed_t[low : low + 128, pl.ds(at, 128)] = out[:, 128 * t : 128 * t + 128].T
             return 0
 
         lax.fori_loop(0, 2, part, 0)
@@ -542,9 +541,6 @@
     norm_block(lambda s_: g.tokens[s_], r)
     lk.got(tok_sib, g.tok_all.at[r_sib])
     norm_block(lambda s_: g.tok_all[r_sib, s_], r_sib)
-    for k in (1, 2, 3):
-        gather_pass(back_g, back_region, k)
-
     lk.got(tok_x, g.tok_all.at[r_xn])
     tok_f = lk.put(g.tok_all.at[r_xn], g.tok_all.at[r_xn], sib)
     norm_block(lambda s_: g.tok_all[r_xn, s_], r_xn)
@@ -568,52 +564,48 @@
         for k in range(1, 8):
             lk.got(slots[k - 1], landing.at[lax.rem(n + 8 - k, 8)])
 
-    def unpack(landing, out, lead):
+    def unpack(landing, put):
         def one(nm, _):
             for tb in range(8):
                 s_, cm = 2 * (tb // 4) + tb % 2, (tb // 2) % 2
-                at = aligned(((32 * s_ + lead) + 2 * nm + cm) * 16, 16)
-                out[pl.ds(at, 16), :] = landing[nm, :, 128 * tb : 128 * tb + 128].astype(f32)
+                put(s_, 2 * nm + cm, landing[nm, :, 128 * tb : 128 * tb + 128].astype(f32))
             return 0
 
         lax.fori_loop(0, 8, one, 0)
+
+    def put_val(s_, i, tile):
+        g.v32[pl.ds(aligned((32 * s_ + 16 + i) * 16, 16), 16), :] = tile
+        g.vr32[pl.ds(aligned((16 * s_ + 15 - i) * 16, 16), 16), :] = tile
+
+    def put_grad(s_, i, tile):
+        g.v32[pl.ds(aligned((32 * s_ + 31 - i) * 16, 16), 16), :] = tile
 
     val_s = channel_send(g.val, g.val_in)
     g.val_in[n] = g.val[pl.ds(aligned(16 * n, 16), 16), :]
-
-    def down_got(zl):
-        for cm in range(2):
-            region = g.w_down_all.at[zl, y, cm]
-            pltpu.make_async_copy(region, region, lk.recv_sems.at[dn_r + 2 * zl + cm]).wait()
-
-    dn_y = []
-    for zl in range(2):
-        down_got(zl)
-        dn_y.append(lk.put(g.w_down_all.at[zl, y], g.w_down_all.at[zl, y], ynb))
+    for i, (to, xm, cm, rm) in enumerate(members):
+        lk.got(up_s[i], g.w_up_all.at[xm, n, cm])
+    up_g = gather_start(up_region)
+    down_pass(1 - dn_first)
 
     zero = jnp.zeros((256, 128), f32)
     for s_ in range(4):
         g.v32[pl.ds(512 * s_, 256), :] = zero
-        g.g32[pl.ds(512 * s_ + 256, 256), :] = zero
     diag_i = lax.broadcasted_iota(jnp.int32, (32, 32), 0) == lax.broadcasted_iota(
         jnp.int32, (32, 32), 1
     )
     skip_row = jnp.broadcast_to(g.skip[...].astype(f32), (32, 32))
     g.skip_b[...] = dot(jnp.where(diag_i, skip_row, 0.0).astype(bf16), jnp.ones((32, 128), bf16))
-
-    lk.got(cot_x, g.cot_all.at[r_xn])
-    cot_f = lk.put(g.cot_all.at[r_xn], g.cot_all.at[r_xn], sib)
+    gather_pass(up_g, up_region, 1)
 
     channel_got(val_s, g.val_in)
-    unpack(g.val_in, g.v32, 16)
+    unpack(g.val_in, put_val)
+
+    def conv_rows(h, k):
+        rows = [g.v32[pl.ds((32 * s_ + 16 - k) * 16 + h, 16, stride=16), :] for s_ in range(4)]
+        return jnp.concatenate(rows, axis=0)
 
     def conv(h, _):
-        parts = []
-        for k in range(16):
-            rows = [
-                g.v32[pl.ds((32 * s_ + 16 - k) * 16 + h, 16, stride=16), :] for s_ in range(4)
-            ]
-            parts.append(jnp.concatenate(rows, axis=0))
+        parts = [conv_rows(h, k) for k in range(16)]
         out = g.skip_b[pl.ds(16 * x + h, 1), :] * parts[0]
         for kk in range(8):
             lhs = jnp.concatenate([parts[2 * kk], parts[2 * kk + 1]], axis=1).astype(bf16)
@@ -621,11 +613,12 @@
         g.o32[pl.ds(h, 64, stride=16), :] = out
         return 0
 
-    def pack(out):
+    def pack(out, back):
         def one(nm, _):
             for tb in range(8):
                 s_, cm = 2 * (tb // 4) + tb % 2, (tb // 2) % 2
-                at = aligned((16 * s_ + 2 * nm + cm) * 16, 16)
+                i = 2 * nm + cm
+                at = aligned((16 * s_ + (15 - i if back else i)) * 16, 16)
                 out[nm, :, 128 * tb : 128 * tb + 128] = g.o32[pl.ds(at, 16), :].astype(bf16)
             return 0
 
@@ -645,67 +638,82 @@
             at = aligned(16 * lax.rem(n + 8 - k, 8), 16)
             lk.got(slots[k - 1], landing.at[pl.ds(at, 16), :])
 
-    lax.fori_loop(0, 16, conv, 0)
-    pack(g.mix_out)
+    lax.fori_loop(0, 16, conv, 0, unroll=2)
+    pack(g.mix_out, False)
     mix_s = channel_back(g.mix_out, g.mix.at[r])
     g.mix[r, pl.ds(aligned(16 * n, 16), 16), :] = g.mix_out[n]
 
-    gather_end(up_g, up_region)
-
-    def up_tile(i, _):
-        rows = pl.ds(aligned(256 * lax.rem(i, 4), 256), 256)
-        at = pl.ds(aligned(256 * (i // 4), 256), 256)
-        w = g.w_up_all[:, :, :, :, at].reshape(1024, 256)
-        act, slope = gelu_parts(dot(g.normed[rows, :], w))
-        g.act[rows, at] = act
-        g.slope[rows, at] = slope
-        return 0
-
-    lax.fori_loop(0, 12, up_tile, 0)
-    channel_back_got(mix_s, g.mix.at[r])
-    mix_sib = lk.put(g.mix.at[r], g.mix.at[r], sib)
-    mix_x = lk.put(g.mix.at[r], g.mix.at[r], xn)
+    gather_pass(up_g, up_region, 2)
+    for i, (to, xm, cm, rm) in enumerate(members):
+        lk.got(back_s[i], g.w_back_all.at[cm, y, xm, z])
+    back_g = gather_start(back_region)
+    lk.got(cot_x, g.cot_all.at[r_xn])
+    cot_f = lk.put(g.cot_all.at[r_xn], g.cot_all.at[r_xn], sib)
+    gather_pass(up_g, up_region, 3)
     for zl in range(2):
-        lk.got(dn_y[zl], g.w_down_all.at[zl, 1 - y])
+        region = g.w_down_all.at[zl, 1 - y]
+        pltpu.make_async_copy(region, region, lk.recv_sems.at[dn_y + zl]).wait()
     lk.got(cot_sib, g.cot_all.at[r_sib])
     lk.got(cot_f, g.cot_all.at[r_diag])
     down2d = g.w_down_all.reshape(768, 1024)
-
-    def hidden_tile(i, _):
-        q = i // 3
-        at = pl.ds(aligned(256 * lax.rem(i, 3), 256), 256)
+    cot2d = g.cot_all.reshape(1024, 1024)
+
+    def hidden_tile(q, _):
         rows = pl.ds(aligned(256 * q, 256), 256)
-        gh = dot_nt(g.cot_all[q].reshape(256, 1024), down2d[at, :])
-        g.g_gate[rows, at] = (gh * g.act[rows, at]).astype(bf16)
-        g.slope[rows, at] = gh * g.slope[rows, at]
+        g.slope[rows, :] = dot_nt(cot2d[rows, :], down2d[...])
         return 0
 
-    lax.fori_loop(0, 12, hidden_tile, 0)
+    lax.fori_loop(0, 4, hidden_tile, 0)
+    channel_back_got(mix_s, g.mix.at[r])
+    mix_x = lk.put(g.mix.at[r], g.mix.at[r], xn)
+    mix_sib = lk.put(g.mix.at[r], g.mix.at[r], sib)
+    gather_pass(back_g, back_region, 1)
+
+    gather_end(up_g, up_region)
+    up2d = g.w_up_all.reshape(1024, 768)
+
+    def up_tile(q, _):
+        rows = pl.ds(aligned(256 * q, 256), 256)
+        act, slope = gelu_parts(dot(g.normed[rows, :], up2d[...]))
+        gh = g.slope[rows, :]
+        g.act[rows, :] = act
+        g.g_gate[rows, :] = (gh * act).astype(bf16)
+        g.slope[rows, :] = gh * slope
+        return 0
+
+    lax.fori_loop(0, 2, up_tile, 0)
+    gather_pass(back_g, back_region, 2)
+    lax.fori_loop(2, 4, up_tile, 0)
+    gather_pass(back_g, back_region, 3)
     lk.got(mix_x, g.mix.at[r_xn])
     mix_f = lk.put(g.mix.at[r_xn], g.mix.at[r_xn], sib)
     gather_end(back_g, back_region)
     back2d = g.w_back_all.reshape(512, 768)
 
-    def mixed_part(xm, cm, q):
-        w = back2d[pl.ds(aligned(128 * (2 * xm + cm), 128), 128), :]
-        return dot_nt(w, g.g_gate[pl.ds(aligned(256 * q, 256), 256), :])
-
-    def gm_sib(i, _):
-        xm, q = i // 4, lax.rem(i, 4)
-        at = pl.ds(aligned(256 * q, 128), 256)
-        g.gm_send[xm, :, at] = mixed_part(xm, 1 - c, q).astype(bf16)
+    def mixed_part(ranks, q):
+        w = [back2d[pl.ds(aligned(128 * rr, 128), 128), :] for rr in ranks]
+        w = w[0] if len(w) == 1 else jnp.concatenate(w, axis=0)
+        return dot_nt(w, g.g_gate[pl.ds(aligned(512 * q, 512), 512), :])
+
+    def gm_sib(q, _):
+        at = pl.ds(aligned(512 * q, 128), 512)
+        both = mixed_part((1 - c, 2 + 1 - c), q).astype(bf16)
+        g.gm_send[:, :, at] = both.reshape(2, 128, 512)
         return 0
 
-    lax.fori_loop(0, 8, gm_sib, 0)
+    lax.fori_loop(0, 2, gm_sib, 0)
     gm_s = lk.put(g.gm_send, g.gm_in, sib)
 
-    def gm_far_add(q, _):
-        at = pl.ds(aligned(256 * q, 128), 256)
-        g.gm_x[:, at] = (mixed_part(1 - x, c, q) + g.gm_in[1 - x, :, at].astype(f32)).astype(bf16)
+    def gm_mine(q, _):
+        at = pl.ds(aligned(512 * q, 128), 512)
+        both = mixed_part((2 * (1 - x) + c, 2 * x + c), q)
+        g.gm_x[:, at] = both[0:128, :].astype(bf16)
+        g.gm_own[:, at] = both[128:256, :]
         return 0
 
+    lax.fori_loop(0, 2, gm_mine, 0)
     lk.got(gm_s, g.gm_in)
-    lax.fori_loop(0, 4, gm_far_add, 0)
+    g.gm_x[...] = (g.gm_x[...].astype(f32) + g.gm_in[1 - x].astype(f32)).astype(bf16)
     gm_xs = lk.put(g.gm_x, g.gm_xin, xn)
 
     lk.got(mix_sib, g.mix.at[r_sib])
@@ -718,76 +726,42 @@
         g.mix_tok[rows, at] = g.mix[rr, :, rows].T
         return 0
 
-    lax.fori_loop(0, 32, turn, 0)
-
-    def gate_tile(i, _):
-        q = i // 3
+    lax.fori_loop(0, 32, turn, 0, unroll=4)
+
+    def gate_tile(q, _):
         rows = pl.ds(aligned(256 * q, 256), 256)
-        at = pl.ds(aligned(256 * lax.rem(i, 3), 256), 256)
-        gate = dot(g.mix_tok[rows, :], back2d[:, at])
-        hidden = (g.act[rows, at] * gate).astype(bf16)
-        g.hidden[rows, at] = hidden
-        g.hidden_t[at, rows] = hidden.T
-        g.g_up[rows, at] = (g.slope[rows, at] * gate).astype(bf16)
+        gate = dot(g.mix_tok[rows, :], back2d[...])
+        hidden = (g.act[rows, :] * gate).astype(bf16)
+        g.hidden[rows, :] = hidden
+        g.hidden_t[:, rows] = hidden.T
+        g.g_up[rows, :] = (g.slope[rows, :] * gate).astype(bf16)
         return 0
 
-    lax.fori_loop(0, 12, gate_tile, 0)
-
-    def gm_own(q, _):
-        at = pl.ds(aligned(256 * q, 128), 256)
-        g.gm[:, at] = (
-            mixed_part(x, c, q) + g.gm_in[x, :, at].astype(f32) + g.gm_xin[:, at].astype(f32)
-        ).astype(bf16)
-        return 0
+    lax.fori_loop(0, 4, gate_tile, 0)
+
+    gd_y = []
+
+    def down_grad(zl):
+        def tile(i, _):
+            at = pl.ds(aligned(512 * i, 512), 512)
+            part = dot(g.hidden_t[384 * zl : 384 * zl + 384, :], cot2d[:, at]).astype(bf16)
+            g.gd[zl, :, :, at] = part.reshape(2, 192, 512)
+            return 0
+
+        lax.fori_loop(0, 2, tile, 0)
+        gd_y.append(lk.put(g.gd.at[zl, 1 - y], g.gd_y.at[zl], ynb))
+
+    down_grad(0)
 
     lk.got(gm_xs, g.gm_xin)
-    lax.fori_loop(0, 4, gm_own, 0)
+    for tb in range(8):
+        at = slice(128 * tb, 128 * tb + 128)
+        total = g.gm_own[:, at] + g.gm_in[x, :, at].astype(f32) + g.gm_xin[:, at].astype(f32)
+        g.gm[:, at] = dot(total.astype(bf16), flip).astype(bf16)
     gm_cs = channel_send(g.gm, g.gm_land)
     g.gm_land[n] = g.gm[pl.ds(aligned(16 * n, 16), 16), :]
 
-    cot2d = g.cot_all.reshape(1024, 1024)
-    gd_y = []
-    for zl in range(2):
-
-        def down_tile(i, _):
-            rows = pl.ds(aligned(384 * zl + 192 * (i // 4), 64), 192)
-            at = pl.ds(aligned(256 * lax.rem(i, 4), 256), 256)
-            g.gd[zl, i // 4, :, at] = dot(g.hidden_t[rows, :], cot2d[:, at]).astype(bf16)
-            return 0
-
-        lax.fori_loop(0, 8, down_tile, 0)
-        gd_y.append(lk.put(g.gd.at[zl, 1 - y], g.gd_y.at[zl], ynb))
-
-    up_y = []
-
-    def up_grad(k):
-        z_d = zo(k)
-        for xm in range(2):
-            t = 4 * xm + z_d
-
-            def tile(i, _):
-                rows = pl.ds(aligned(128 * t, 128), 128)
-                at = pl.ds(aligned(256 * i, 256), 256)
-                g.gu[xm, z_d, :, at] = dot(g.normed_t[rows, :], g.g_up[:, at]).astype(bf16)
-                return 0
-
-            lax.fori_loop(0, 3, tile, 0)
-            other = pl.ds(aligned(64 * (1 - y), 64), 64)
-            up_y.append((t, lk.put(g.gu.at[xm, z_d, other], g.gu_y.at[t], ynb)))
-
-    own64 = pl.ds(aligned(64 * y, 64), 64)
-    gu_s = {}
-
-    def up_sum(i, k):
-        z_d = zo(k)
-        for xm in range(2):
-            t, slot = up_y[2 * i + xm]
-            lk.got(slot, g.gu_y.at[t])
-            total = g.gu[xm, z_d, own64, :].astype(f32) + g.gu_y[t].astype(f32)
-            g.gu[xm, z_d, own64, :] = total.astype(bf16)
-        if k:
-            gu_s[k] = lk.put(g.gu.at[:, z_d, own64], g.gu_in.at[k - 1], dev(x, z_d, y, c))
-
+    down_grad(1)
     gd_r = lk.take(4)
 
     def down_sum(zl):
@@ -802,96 +776,82 @@
                 g.gd.at[zl, y, part], g.gd_in.at[z], lk.take(), gd_r + z, dev(x, z_d, y, cm), here
             )
 
-    up_grad(1)
+    channel_got(gm_cs, g.gm_land)
+    unpack(g.gm_land, put_grad)
     down_sum(0)
-    up_grad(2)
-    down_sum(1)
-    up_sum(0, 1)
-    up_grad(3)
-    up_sum(1, 2)
-    up_grad(0)
-    up_sum(2, 3)
-
-    mix2d = g.mix.reshape(512, 1024)
-
-    def back_tile(rr):
-        def tile(i, _):
-            at = pl.ds(aligned(256 * i, 256), 256)
-            rows = pl.ds(aligned(128 * rr, 128), 128)
-            g.gb[rr // 2, lax.rem(rr, 2), :, at] = dot(
-                mix2d[rows, :], g.g_gate[:, at]
-            ).astype(bf16)
-            return 0
-
-        lax.fori_loop(0, 3, tile, 0)
-
-    gb_y = []
-    for cm in range(2):
-        back_tile(2 * cm + 1 - y)
-        gb_y.append(lk.put(g.gb.at[cm, 1 - y], g.gb_y.at[cm], ynb))
-    up_sum(3, 0)
-    for cm in range(2):
-        back_tile(2 * cm + y)
-
-    channel_got(gm_cs, g.gm_land)
-    unpack(g.gm_land, g.g32, 0)
-    g.xs[:, 2048:2176] = jnp.zeros((128, 128), f32)
 
     def conv_back(h, _):
-        parts = []
-        for k in range(16):
-            rows = [g.g32[pl.ds((32 * s_ + k) * 16 + h, 16, stride=16), :] for s_ in range(4)]
-            parts.append(jnp.concatenate(rows, axis=0))
-        own = [g.v32[pl.ds((32 * s_ + 16) * 16 + h, 16, stride=16), :] for s_ in range(4)]
-        own = jnp.concatenate(own, axis=0)
-        g.skip_part[pl.ds(h, 1), :] = jnp.sum(own * parts[0], axis=0, keepdims=True)
-        own_t = own.T.astype(bf16)
+        parts = [conv_rows(h, k) for k in range(16)]
+        own = g.vr32[pl.ds(h, 64, stride=16), :].T.astype(bf16)
         out = g.skip_b[pl.ds(16 * x + h, 1), :] * parts[0]
+        lhs = []
         for kk in range(8):
-            lhs = jnp.concatenate([parts[2 * kk], parts[2 * kk + 1]], axis=1).astype(bf16)
-            rhs = jnp.concatenate([g.toep[h, 2 * kk], g.toep[h, 2 * kk + 1]], axis=1)
-            out = out + dot_nt(lhs, rhs)
-            g.xs[:, 256 * kk : 256 * kk + 256] = dot(own_t, lhs)
+            lhs.append(jnp.concatenate([parts[2 * kk], parts[2 * kk + 1]], axis=1).astype(bf16))
+            out = out + dot(lhs[kk], g.toep[h, 2 * kk : 2 * kk + 2].reshape(256, 128))
         g.o32[pl.ds(h, 64, stride=16), :] = out
-
-        acc = g.xs[120:128, :]
-        for b in range(14, -1, -1):
-            acc = pltpu.roll(acc, 2176 - 8, 1) + g.xs[8 * b : 8 * b + 8, :]
-        for k in range(17):
-            at = pl.ds(aligned(128 * k + 8 * h, 8), 8)
-            g.gk8[at, :] = acc[:, 128 * k : 128 * k + 128]
+        after = jnp.zeros((128, 128), f32)
+        for kk in range(7, -1, -1):
+            pair = dot(own, lhs[kk])
+            for half in (1, 0):
+                turned = pltpu.roll(
+                    pair[:, 128 * half : 128 * half + 128], 0, 1, stride=1, stride_axis=0
+                )
+                lag = jnp.where(jj >= ii, turned, after)
+                after = turned
+                at = pl.ds(aligned((16 * (2 * kk + half) + h) * 8, 8), 8)
+                g.gk8[at, :] = jnp.sum(lag.reshape(16, 8, 128), axis=0)
         return 0
 
     lax.fori_loop(0, 16, conv_back, 0)
-    pack(g.gv_out)
+    pack(g.gv_out, True)
     gv_s = channel_back(g.gv_out, g.g_val)
     g.g_val[pl.ds(aligned(16 * n, 16), 16), :] = g.gv_out[n]
 
-    for cm in range(2):
-        lk.got(gb_y[cm], g.gb_y.at[cm])
-        total = g.gb[cm, y].astype(f32) + g.gb_y[cm].astype(f32)
-        g.gb_z[pl.ds(2 * cm, 2)] = total.astype(bf16).reshape(2, 4, 16, 768)
-    gb_s = {}
-    for k in (1, 2, 3):
-        gb_s[k] = lk.put(g.gb_z.at[:, zo(k)], g.gb_in.at[k - 1], dev(x, zo(k), y, c))
-
-
-    def gk_rows(s_):
-        tiles = [g.gk8[pl.ds(128 * k + s_, 16, stride=8), :] for k in range(17)]
-        return jnp.concatenate(tiles, axis=1)
-
-    acc = gk_rows(7)
-    for s_ in range(6, -1, -1):
-        acc = pltpu.roll(acc, 2176 - 1, 1) + gk_rows(s_)
-    g.gk[...] = acc
+    other = pl.ds(aligned(64 * (1 - y), 64), 64)
+    own64 = pl.ds(aligned(64 * y, 64), 64)
+    up_y, gu_s = {}, {}
+
+    def up_grad(k):
+        z_d = zo(k)
+        rows = pl.ds(aligned(256 * z_d, 256), 256)
+        part = dot(g.normed_t[rows, :], g.g_up[...]).astype(bf16)
+        g.gu[z_d] = part.reshape(2, 128, 768)
+        up_y[k] = lk.put(g.gu.at[z_d, :, other], g.gu_y.at[z_d], ynb)
+
+    def up_sum(k):
+        z_d = zo(k)
+        lk.got(up_y[k], g.gu_y.at[z_d])
+        total = g.gu[z_d, :, own64, :].astype(f32) + g.gu_y[z_d].astype(f32)
+        g.gu[z_d, :, own64, :] = total.astype(bf16)
+        if k:
+            gu_s[k] = lk.put(g.gu.at[z_d, :, own64], g.gu_in.at[k - 1], dev(x, z_d, y, c))
+
+    up_grad(2)
+    up_grad(1)
+    up_grad(3)
+    up_grad(0)
+    down_sum(1)
+
+    mix2d = g.mix.reshape(512, 1024)
+
+    def back_tile(i, _):
+        at = pl.ds(aligned(384 * i, 128), 384)
+        part = dot(mix2d[...], g.g_gate[:, at]).astype(bf16)
+        g.gb[:, :, :, at] = part.reshape(2, 2, 128, 384)
+        return 0
+
+    lax.fori_loop(0, 2, back_tile, 0)
+    gb_y = lk.put(g.gb.at[:, 1 - y], g.gb_y, ynb)
+
+    tall = g.gk8[pl.ds(0, 256, stride=8), :]
+    for s_ in range(1, 8):
+        tall = tall + g.gk8[pl.ds(s_, 256, stride=8), :]
     for half in range(2):
-        tall = jnp.concatenate(
-            [g.gk[:, 128 * k : 128 * k + 128] for k in range(8 * half, 8 * half + 8)], axis=0
-        )
-        hi_, lo_ = split(tall)
+        hi_, lo_ = split(tall[128 * half : 128 * half + 128, :])
         g.state[128 * half : 128 * half + 128, :] = (
             dot(hi_, g.near_t_hi[...]) + dot(lo_, g.near_t_hi[...]) + dot(hi_, g.near_t_lo[...])
         )
+    g.skip_sum[...] = tall[0:16, :]
 
     def far_back(p, carry):
         gc, gs = carry
@@ -907,141 +867,65 @@
     g.gcoef[0] = gc
     g.gcoef[1] = gs
     gcoef_s = lk.put(g.gcoef.at[1 - x], g.gcoef_in, xn)
-    g.skip_sum[...] = jnp.broadcast_to(jnp.sum(g.skip_part[...], axis=1, keepdims=True), (16, 128))
     skip_s = lk.put(g.skip_sum, g.skip_in, xn)
 
+    channel_back_got(gv_s, g.g_val)
+    for tb in range(8):
+        at = slice(128 * tb, 128 * tb + 128)
+        back = dot(g.g_val[:, at], flip)
+        g.gvp_t[at, :] = (back * g.val_slope[:, at]).astype(bf16).T
+    part = dot(g.normed_t[...], g.gvp_t[...]).astype(bf16)
+    g.gv[...] = part.reshape(4, 2, 128, 128)
+    gv_y = lk.put(g.gv.at[:, :, other], g.gv_y, ynb)
+
     def group_sum(part, send, land, xsend, xland):
-        def to_sib(i, _):
-            xm, j = i // 4, lax.rem(i, 4)
-            at = pl.ds(aligned(256 * j, 256), 256)
-            send[xm, :, at] = part(xm, 1 - c, at).astype(bf16)
-            return 0
-
-        lax.fori_loop(0, 8, to_sib, 0)
+        for xm in range(2):
+            send[xm] = part(xm, 1 - c).astype(bf16)
         first = lk.put(send, land, sib)
-
-        def add_far(j, _):
-            at = pl.ds(aligned(256 * j, 256), 256)
-            xsend[:, at] = (part(1 - x, c, at) + land[1 - x, :, at].astype(f32)).astype(bf16)
-            return 0
-
+        mine = part(1 - x, c)
         lk.got(first, land)
-        lax.fori_loop(0, 4, add_far, 0)
+        xsend[...] = (mine + land[1 - x].astype(f32)).astype(bf16)
         second = lk.put(xsend, xland, xn)
 
-        def own(at):
-            return part(x, c, at) + land[x, :, at].astype(f32) + xland[:, at].astype(f32)
+        def own():
+            return part(x, c) + land[x].astype(f32) + xland[...].astype(f32)
 
         return second, own
 
+    def branch_part(xm, cm):
+        rows = pl.ds(aligned(256 * (2 * xm + cm), 256), 256)
+        return dot(g.hidden[rows, :], down2d[...])
+
+    def normed_part(xm, cm):
+        rows = pl.ds(aligned(256 * (2 * xm + cm), 256), 256)
+        return dot_nt(g.g_up[rows, :], up2d[...]) + dot_nt(g.gvp_t[rows, :], g.w_val[...])
+
     spare = g.normed.reshape(2, 2, 256, 1024)
-
-    def branch_part(xm, cm, at):
-        rows = pl.ds(aligned(256 * (2 * xm + cm), 256), 256)
-        return dot(g.hidden[rows, :], down2d[:, at])
-
+    gn_s, gn_own = group_sum(
+        normed_part, spare.at[1], g.gn_in, g.tok_all.at[r_sib].reshape(256, 1024), g.gn_xin
+    )
+    up_sum(2)
+    up_sum(1)
     br_s, br_own = group_sum(
         branch_part, spare.at[0], g.br_in, g.tok_all.at[r].reshape(256, 1024), g.br_xin
     )
-
-    channel_back_got(gv_s, g.g_val)
-    gvp = (g.g_val[...].astype(f32) * g.val_slope[...]).astype(bf16)
-    g.gvp_t[...] = gvp.T
-
-    def val_tile(t, _):
-        rows = pl.ds(aligned(128 * t, 128), 128)
-        g.gv[t] = dot(g.normed_t[rows, :], g.gvp_t[...]).astype(bf16)
-        return 0
-
-    lax.fori_loop(0, 8, val_tile, 0)
-    other = pl.ds(aligned(64 * (1 - y), 64), 64)
-    gv_y = lk.put(g.gv.at[:, other], g.gv_y, ynb)
-
-    up2d = g.w_up_all.reshape(1024, 768)
-
-    def normed_part(xm, cm, at):
-        rows = pl.ds(aligned(256 * (2 * xm + cm), 256), 256)
-        return dot_nt(g.g_up[rows, :], up2d[at, :]) + dot_nt(g.gvp_t[rows, :], g.w_val[at, :])
-
-    gn_s, gn_own = group_sum(
-        normed_part, spare.at[1], g.gn_in, g.tok_all.at[r_sib].reshape(256, 1024), g.gn_xin
-    )
-
+    up_sum(3)
+    up_sum(0)
+
+    lk.got(gb_y, g.gb_y)
+    total = g.gb[:, y].astype(f32) + g.gb_y[...].astype(f32)
+    g.gb_z[...] = total.astype(bf16).reshape(4, 4, 16, 768)
+    gb_s = {}
+    for k in (2, 1, 3):
+        gb_s[k] = lk.put(g.gb_z.at[:, zo(k)], g.gb_in.at[k - 1], dev(x, zo(k), y, c))
     lk.got(gv_y, g.gv_y)
-    total = (g.gv[:, own64, :].astype(f32) + g.gv_y[...].astype(f32)).astype(bf16)
-    g.gv_z[...] = total.reshape(2, 4, 64, 128)
+    g.gv_z[...] = (g.gv[:, :, own64, :].astype(f32) + g.gv_y[...].astype(f32)).astype(bf16)
     gv_zs = {}
-    for k in (1, 2, 3):
-        gv_zs[k] = lk.put(g.gv_z.at[:, zo(k)], g.gv_in.at[k - 1], dev(x, zo(k), y, c))
-
-    for k in (1, 2, 3):
-        lk.got(gu_s[k], g.gu_in.at[k - 1])
-    total = g.gu[:, z, own64, :].astype(f32)
-    for k in range(3):
-        total = total + g.gu_in[k].astype(f32)
-    g.gu_f[...] = total.reshape(2, 2, 32, 768).astype(bf16)
-    for k in (1, 2, 3):
-        lk.got(gb_s[k], g.gb_in.at[k - 1])
-    total = g.gb_z[:, z].astype(f32)
-    for k in range(3):
-        total = total + g.gb_in[k].astype(f32)
-    g.gb_f[...] = total.astype(bf16)
-    fin_u = [lk.put(g.gu_f.at[xm, cm], g.fu_in.at[r], to) for to, xm, cm, rm in members]
-    fin_b = [lk.put(g.gb_f.at[2 * cm + xm], g.fb_in.at[r], to) for to, xm, cm, rm in members]
-    g.fu_in[r] = g.gu_f[x, c]
-    g.fb_in[r] = g.gb_f[2 * c + x]
-
-    lk.got(br_s, g.br_xin)
-
-    def result_tile(j, _):
-        at = pl.ds(aligned(256 * j, 256), 256)
-        out = br_own(at).reshape(2, 128, 256) + g.tokens[:, :, at].astype(f32)
-        g.result[:, :, at] = out.astype(bf16)
-        return 0
-
-    lax.fori_loop(0, 4, result_tile, 0)
-
-    for zs in range(4):
-        region = g.gd_in.at[zs]
-        pltpu.make_async_copy(region, region, lk.recv_sems.at[gd_r + zs]).wait()
-    total = g.gd_in[0].astype(f32)
-    for zs in range(1, 4):
-        total = total + g.gd_in[zs].astype(f32)
-    g.o_down[...] = total
-
-    for k in (1, 2, 3):
-        lk.got(gv_zs[k], g.gv_in.at[k - 1])
-    total = g.gv_z[:, z].astype(f32)
-    for k in range(3):
-        total = total + g.gv_in[k].astype(f32)
-    g.gv_f[...] = total.reshape(2, 2, 32, 128).astype(bf16)
-    fin_v = [lk.put(g.gv_f.at[xm, cm], g.fv_in.at[r], to) for to, xm, cm, rm in members]
-    g.fv_in[r] = g.gv_f[x, c]
-
-    mine = pl.ds(aligned(16 * x, 16), 16)
-    theirs = pl.ds(aligned(16 * (1 - x), 16), 16)
-    lk.got(gcoef_s, g.gcoef_in)
-    g.o_coef[mine, :] = g.gcoef[x]
-    g.o_coef[theirs, :] = g.gcoef_in[...]
-    lk.got(skip_s, g.skip_in)
-    g.o_skip[mine, :] = g.skip_sum[...]
-    g.o_skip[theirs, :] = g.skip_in[...]
-
-    for i, (to, xm, cm, rm) in enumerate(members):
-        lk.got(fin_u[i], g.fu_in.at[rm])
-        lk.got(fin_b[i], g.fb_in.at[rm])
-    for rr in range(4):
-        g.o_up[:, 768 * rr : 768 * rr + 768] = g.fu_in[rr].astype(f32)
-        g.o_back[:, 768 * rr : 768 * rr + 768] = g.fb_in[rr].astype(f32)
+    for k in (2, 1, 3):
+        gv_zs[k] = lk.put(g.gv_z.at[zo(k)], g.gv_in.at[k - 1], dev(x, zo(k), y, c))
 
     lk.got(gn_s, g.gn_xin)
-
-    def gn_tile(j, _):
-        at = pl.ds(aligned(256 * j, 256), 256)
-        g.state[:, at] = gn_own(at)
-        return 0
-
-    lax.fori_loop(0, 4, gn_tile, 0)
+    g.state[...] = gn_own()
 
     def norm_back(i, carry):
         dg, ds = carry
@@ -1073,16 +957,69 @@
     for k in range(1, 8):
         to = lax.rem(n + k, 8)
         ng_s.append(lk.put(g.ng.at[to // 2], g.ng_in.at[k - 1], (x, 2 * to + c)))
-    for i, (to, xm, cm, rm) in enumerate(members):
-        lk.got(fin_v[i], g.fv_in.at[rm])
-    wide = jnp.concatenate([g.fv_in[rr] for rr in range(4)], axis=1)
-    g.o_value[...] = dot_nt(wide, g.perm[...])
+
+    lk.got(br_s, g.br_xin)
+    out = br_own().reshape(2, 128, 1024) + g.tokens[...].astype(f32)
+    g.result[...] = out.astype(bf16)
+
+    for k in (2, 1, 3):
+        lk.got(gu_s[k], g.gu_in.at[k - 1])
+    total = g.gu[z, :, own64, :].astype(f32)
+    for k in range(3):
+        total = total + g.gu_in[k].astype(f32)
+    g.gu_f[...] = total.reshape(2, 2, 32, 768).astype(bf16)
+    fin_u = [lk.put(g.gu_f.at[xm, cm], g.fu_in.at[r], to) for to, xm, cm, rm in members]
+    for k in (2, 1, 3):
+        lk.got(gb_s[k], g.gb_in.at[k - 1])
+    total = g.gb_z[:, z].astype(f32)
+    for k in range(3):
+        total = total + g.gb_in[k].astype(f32)
+    g.gb_f[...] = total.astype(bf16)
+    fin_b = [lk.put(g.gb_f.at[2 * cm + xm], g.fb_in.at[r], to) for to, xm, cm, rm in members]
+    for k in (2, 1, 3):
+        lk.got(gv_zs[k], g.gv_in.at[k - 1])
+    total = g.gv_z[z].astype(f32)
+    for k in range(3):
+        total = total + g.gv_in[k].astype(f32)
+    g.gv_f[...] = total.reshape(2, 2, 32, 128).astype(bf16)
+    fin_v = [lk.put(g.gv_f.at[xm, cm], g.fv_in.at[r], to) for to, xm, cm, rm in members]
+    g.fu_in[r] = g.gu_f[x, c]
+    g.fb_in[r] = g.gb_f[2 * c + x]
+    g.fv_in[r] = g.gv_f[x, c]
+
+    for zs in range(4):
+        region = g.gd_in.at[zs]
+        pltpu.make_async_copy(region, region, lk.recv_sems.at[gd_r + zs]).wait()
+    total = g.gd_in[0].astype(f32)
+    for zs in range(1, 4):
+        total = total + g.gd_in[zs].astype(f32)
+    g.o_down[...] = total
+
+    mine = pl.ds(aligned(16 * x, 16), 16)
+    theirs = pl.ds(aligned(16 * (1 - x), 16), 16)
+    lk.got(gcoef_s, g.gcoef_in)
+    g.o_coef[mine, :] = g.gcoef[x]
+    g.o_coef[theirs, :] = g.gcoef_in[...]
+    lk.got(skip_s, g.skip_in)
+    g.o_skip[mine, :] = g.skip_sum[...]
+    g.o_skip[theirs, :] = g.skip_in[...]
+
     total = g.ng[z]
     for k in range(1, 8):
         lk.got(ng_s[k - 1], g.ng_in.at[k - 1])
         total = total + g.ng_in[k - 1]
     g.ng_f[...] = total
     ng_t = [lk.put(g.ng_f, g.ng_fin.at[i], to) for i, (to, xm, cm, rm) in enumerate(members)]
+
+    for i, (to, xm, cm, rm) in enumerate(members):
+        lk.got(fin_u[i], g.fu_in.at[rm])
+        lk.got(fin_b[i], g.fb_in.at[rm])
+        lk.got(fin_v[i], g.fv_in.at[rm])
+    for rr in range(4):
+        g.o_up[:, 768 * rr : 768 * rr + 768] = g.fu_in[rr].astype(f32)
+        g.o_back[:, 768 * rr : 768 * rr + 768] = g.fb_in[rr].astype(f32)
+    wide = jnp.concatenate([g.fv_in[rr] for rr in range(4)], axis=1)
+    g.o_value[...] = dot_nt(wide, g.perm[...])
     for i in range(3):
         lk.got(ng_t[i], g.ng_fin.at[i])
         total = total + g.ng_fin[i]
@@ -1154,7 +1091,7 @@
         val=((128, 1024), bf16),
         val_in=((8, 16, 1024), bf16),
         v32=((2048, 128), f32),
-        g32=((2048, 128), f32),
+        vr32=((1024, 128), f32),
         o32=((1024, 128), f32),
         skip_b=((32, 128), f32),
         mix_out=((8, 16, 1024), bf16),
@@ -1175,8 +1112,8 @@
         gd=((2, 2, 192, 1024), bf16),
         gd_y=((2, 192, 1024), bf16),
         gd_in=((4, 96, 1024), bf16),
-        gu=((2, 4, 128, 768), bf16),
-        gu_y=((8, 64, 768), bf16),
+        gu=((4, 2, 128, 768), bf16),
+        gu_y=((4, 2, 64, 768), bf16),
         gu_in=((3, 2, 64, 768), bf16),
         gu_f=((2, 2, 32, 768), bf16),
         fu_in=((4, 32, 768), bf16),
@@ -1186,16 +1123,14 @@
         gb_in=((3, 4, 16, 768), bf16),
         gb_f=((4, 16, 768), bf16),
         fb_in=((4, 16, 768), bf16),
-        gv=((8, 128, 128), bf16),
-        gv_y=((8, 64, 128), bf16),
-        gv_z=((2, 4, 64, 128), bf16),
+        gv=((4, 2, 128, 128), bf16),
+        gv_y=((4, 2, 64, 128), bf16),
+        gv_z=((4, 2, 64, 128), bf16),
         gv_in=((3, 2, 64, 128), bf16),
         gv_f=((2, 2, 32, 128), bf16),
         fv_in=((4, 32, 128), bf16),
-        xs=((128, 2176), f32),
-        gk8=((2176, 128), f32),
-        gk=((16, 2176), f32),
-        skip_part=((16, 128), f32),
+        gk8=((2048, 128), f32),
+        gm_own=((128, 1024), f32),
         skip_sum=((16, 128), f32),
         skip_in=((16, 128), f32),
         gcoef=((2, 16, 512), f32),
@@ -1236,7 +1171,7 @@
         o.o_back,
         o.o_down,
         o.o_coef,
-        o.o_skip[:, 0],
+        o.o_skip[:, 127],
     )
 
 

time: 237 us -> 181 us (0.76)
  Pallas kernels: 227 us -> 170 us
    pallas_call x1, Pallas kernels: 227 us -> 170 us  [fast_body(): pl.pallas_call(functools.partial(layer_kernel, names), out_shape=[jax.Sha...]
where the time goes in v2:
time: 181 us; the launch traced here: 180 us
  Pallas kernels  170 us (94%)
  local copies, waits for them, and re-layouts  9.53 us (5%)
    pallas_call x1, Pallas kernels, fast_body(): pl.pallas_call(functools.partial(layer_kernel, names), out_shape=[jax.Sha...  170 us
    unnamed x19, local copies, waits for them, and re-layouts  6.77 us

profile of v2, /device:TPU:0, one launch (start us, length us, event | category | flops | bytes accessed | tf_op | source)
XLA Modules:
  0.0 180.4 jit_solution(17204057761589005227)
XLA Ops:
  0.6 170.2 %shard_map.231 = (bf16[2,128,1024]{2,1,0:T(8,128)(2,1)}, f32[2,128,1024]{2,1,0:T(8,128)}, f32[8,128]{1,0:T(8,128)}, f32[32,3072]{1,0:T(8,128)}, f32[32,512]{1,0:...) custom-call(bf16[2,128,1024]{2,1,0:T(8,128)(2,1)} %refs_0_.1, ...), custom_call_target="tpu_custom_call" | custom-call | tf_op jit(solution)/shard_map/pallas_call | solution.py:1152
  170.9 0.0 copy-start
  170.9 1.5 slice_reduce_fusion
  172.4 1.3 slice_bitcast_fusion
  173.7 1.9 %copy.33 = bf16[2,128,1024]{2,1,0:T(8,128)(2,1)} copy(bf16[2,128,1024]{2,1,0:T(8,128)(2,1)} %get-tuple-element.40) | data formatting | bytes 1048576
  175.5 0.0 copy-done
  175.5 0.0 copy-start.2
  175.5 1.0 copy.34
  176.5 0.3 copy-done.2
  176.8 0.0 copy-start.5
  176.8 0.0 copy-start.3
  176.8 0.7 copy.35
  177.5 0.1 copy-done.5
  177.6 0.0 copy-start.1
  177.6 0.6 copy.36
  178.3 0.0 copy-done.3
  178.3 0.7 copy.37
  178.9 0.0 copy-done.1
  178.9 0.0 copy-start.4
  178.9 0.7 copy.38
  179.7 0.1 copy-done.4
  179.8 0.6 copy.39
Async XLA Ops:
  170.9 4.6 %copy-start = (f32[2,128,1024]{2,1,0:T(8,128)S(1)}, f32[2,128,1024]{2,1,0:T(8,128)}, u32[]{:S(2)}) copy-start(f32[2,128,1024]{2,1,0:T(8,128)} %get-tuple-element.41) | copy-start | bytes 3145732
  175.5 1.2 copy-start.2
  176.8 0.9 copy-start.5
  176.8 1.5 copy-start.3
  177.6 1.3 copy-start.1
  178.9 0.9 copy-start.4

commit v3 on v2

--- a/solution.py
+++ b/solution.py
@@ -435,24 +435,73 @@
         lk.got(pk_s[i], g.pk.at[xm, n, cm])
     pk_g = gather_start(pk_region)
 
-    dn_r = lk.take(4)
-    dn_slot = dn_r + 2 * lax.rem(z, 2) + c
+    def line(region, has):
+        right, left, across = lk.take(3), lk.take(3), lk.take(4)
+        passes = lk.take(3)
+
+        def send(zs, ssem, rsem, to, when):
+            copy = lk.make(region(zs, y), region(zs, y), ssem, rsem, to)
+            pl.when(when)(copy.start)
+            lk.pending.append((copy, when))
+
+        def also(when, zs):
+            return when if has is None else jnp.logical_and(when, has(zs))
+
+        def step(k):
+            for way, base in ((-1, right), (1, left)):
+                if k == 0 and way == 1:
+                    continue
+                zs = z + way * k
+                there = also(z >= k if way == -1 else z + k <= 3, zs)
+                if k:
+                    slot = base + k - 1
+                    block = region(lax.rem(zs + 4, 4), y)
+                    wait = lk.make(block, block, slot, slot, ynb)
+                    pl.when(there)(wait.wait_recv)
+                zs = lax.rem(zs + 4, 4)
+                if k < 3 and (way == -1 or k == 0):
+                    on = jnp.logical_and(there, z < 3)
+                    send(zs, right + k, right + k, dev(x, zo(1), y, c), on)
+                if k < 3 and (way == 1 or k == 0):
+                    on = jnp.logical_and(there, z > 0)
+                    send(zs, left + k, left + k, dev(x, zb(1), y, c), on)
+                ssem = across + k if way == -1 else passes + k - 1
+                send(zs, ssem, across + zs, ynb, there)
+
+        def end():
+            for zs in range(4):
+                block = region(zs, 1 - y)
+                wait = lk.make(block, block, across + zs, across + zs, ynb)
+                if has is None:
+                    wait.wait_recv()
+                else:
+                    pl.when(has(zs))(wait.wait_recv)
+
+        return step, end
+
+    def down_region(z_, y_):
+        return g.w_down_all.at[lax.rem(z_, 2), y_]
+
+    def down_has(z_):
+        return (z_ + 4) // 2 == c + 2
+
+    owner = z // 2
+    dn_own = lk.take()
     dst = g.w_down_all.at[lax.rem(z, 2), y, c]
-    owner = z // 2
-    lk.put_or_keep(g.w_down, dst, lk.take(), dn_slot, dev(x, z, y, owner), owner == c)
-    for k in (1, 2, 3):
-        lk.pending.append(
-            (start_of(lk.make(g.w_down, dst, lk.take(), dn_slot, dev(x, zo(k), y, owner))), None)
-        )
-    dn_first = jnp.where(owner == c, lax.rem(z, 2), 1 - c)
-    dn_y = lk.take(2)
-
-    def down_pass(zl):
-        for cm in range(2):
-            region = g.w_down_all.at[zl, y, cm]
-            pltpu.make_async_copy(region, region, lk.recv_sems.at[dn_r + 2 * zl + cm]).wait()
-        region = g.w_down_all.at[zl, y]
-        lk.pending.append((start_of(lk.make(region, region, lk.take(), dn_y + zl, ynb)), None))
+    dn_copy = lk.make(g.w_down, dst, dn_own, dn_own, sib)
+    pl.when(owner != c)(dn_copy.start)
+    lk.pending.append((dn_copy, owner != c))
+
+    @pl.when(owner == c)
+    def _():
+        g.w_down_all[lax.rem(z, 2), y, c] = g.w_down[...]
+        block = g.w_down_all.at[lax.rem(z, 2), y, 1 - c]
+        lk.make(block, block, dn_own, dn_own, sib).wait_recv()
+
+    down_step, down_end = line(down_region, down_has)
+    up_step, up_end = line(up_region, None)
+    back_step, back_end = line(back_region, None)
+    down_step(0)
 
     lk.got(coef_s, g.coef.at[1 - x])
     cc = g.coef[0].astype(f32)
@@ -475,6 +524,7 @@
         )
     for k in (1, 2, 3):
         gather_pass(pk_g, pk_region, k)
+    down_step(1)
     ii = lax.broadcasted_iota(jnp.int32, (128, 128), 0)
     jj = lax.broadcasted_iota(jnp.int32, (128, 128), 1)
     flip = (ii + jj == 127).astype(bf16)
@@ -488,8 +538,7 @@
             prev = turned
         return 0
 
-    lax.fori_loop(0, 16, toeplitz, 0)
-    down_pass(dn_first)
+    lax.fori_loop(0, 16, toeplitz, 0, unroll=2)
 
     gather_end(pk_g, pk_region)
     e_i = lax.broadcasted_iota(jnp.int32, (128, 1024), 0)
@@ -541,6 +590,7 @@
     norm_block(lambda s_: g.tokens[s_], r)
     lk.got(tok_sib, g.tok_all.at[r_sib])
     norm_block(lambda s_: g.tok_all[r_sib, s_], r_sib)
+    down_step(2)
     lk.got(tok_x, g.tok_all.at[r_xn])
     tok_f = lk.put(g.tok_all.at[r_xn], g.tok_all.at[r_xn], sib)
     norm_block(lambda s_: g.tok_all[r_xn, s_], r_xn)
@@ -574,34 +624,34 @@
         lax.fori_loop(0, 8, one, 0)
 
     def put_val(s_, i, tile):
-        g.v32[pl.ds(aligned((32 * s_ + 16 + i) * 16, 16), 16), :] = tile
-        g.vr32[pl.ds(aligned((16 * s_ + 15 - i) * 16, 16), 16), :] = tile
+        g.v32[pl.ds(32 * s_ + 16 + i, 16, stride=128), :] = tile
+        g.vr32[pl.ds(16 * s_ + 15 - i, 16, stride=64), :] = tile
 
     def put_grad(s_, i, tile):
-        g.v32[pl.ds(aligned((32 * s_ + 31 - i) * 16, 16), 16), :] = tile
+        g.v32[pl.ds(32 * s_ + 31 - i, 16, stride=128), :] = tile
 
     val_s = channel_send(g.val, g.val_in)
     g.val_in[n] = g.val[pl.ds(aligned(16 * n, 16), 16), :]
     for i, (to, xm, cm, rm) in enumerate(members):
         lk.got(up_s[i], g.w_up_all.at[xm, n, cm])
-    up_g = gather_start(up_region)
-    down_pass(1 - dn_first)
-
-    zero = jnp.zeros((256, 128), f32)
-    for s_ in range(4):
-        g.v32[pl.ds(512 * s_, 256), :] = zero
+    up_step(0)
+    down_step(3)
+
+    zero = jnp.zeros((16, 128), f32)
+    for i in range(64):
+        g.v32[32 * i : 32 * i + 16, :] = zero
     diag_i = lax.broadcasted_iota(jnp.int32, (32, 32), 0) == lax.broadcasted_iota(
         jnp.int32, (32, 32), 1
     )
     skip_row = jnp.broadcast_to(g.skip[...].astype(f32), (32, 32))
     g.skip_b[...] = dot(jnp.where(diag_i, skip_row, 0.0).astype(bf16), jnp.ones((32, 128), bf16))
-    gather_pass(up_g, up_region, 1)
 
     channel_got(val_s, g.val_in)
     unpack(g.val_in, put_val)
+    up_step(1)
 
     def conv_rows(h, k):
-        rows = [g.v32[pl.ds((32 * s_ + 16 - k) * 16 + h, 16, stride=16), :] for s_ in range(4)]
+        rows = [g.v32[pl.ds(128 * h + 32 * s_ + 16 - k, 16), :] for s_ in range(4)]
         return jnp.concatenate(rows, axis=0)
 
     def conv(h, _):
@@ -610,7 +660,7 @@
         for kk in range(8):
             lhs = jnp.concatenate([parts[2 * kk], parts[2 * kk + 1]], axis=1).astype(bf16)
             out = out + dot(lhs, g.toep[h, 2 * kk : 2 * kk + 2].reshape(256, 128))
-        g.o32[pl.ds(h, 64, stride=16), :] = out
+        g.o32[pl.ds(aligned(64 * h, 64), 64), :] = out
         return 0
 
     def pack(out, back):
@@ -618,8 +668,8 @@
             for tb in range(8):
                 s_, cm = 2 * (tb // 4) + tb % 2, (tb // 2) % 2
                 i = 2 * nm + cm
-                at = aligned((16 * s_ + (15 - i if back else i)) * 16, 16)
-                out[nm, :, 128 * tb : 128 * tb + 128] = g.o32[pl.ds(at, 16), :].astype(bf16)
+                at = pl.ds(16 * s_ + (15 - i if back else i), 16, stride=64)
+                out[nm, :, 128 * tb : 128 * tb + 128] = g.o32[at, :].astype(bf16)
             return 0
 
         lax.fori_loop(0, 8, one, 0)
@@ -643,16 +693,13 @@
     mix_s = channel_back(g.mix_out, g.mix.at[r])
     g.mix[r, pl.ds(aligned(16 * n, 16), 16), :] = g.mix_out[n]
 
-    gather_pass(up_g, up_region, 2)
+    up_step(2)
     for i, (to, xm, cm, rm) in enumerate(members):
         lk.got(back_s[i], g.w_back_all.at[cm, y, xm, z])
-    back_g = gather_start(back_region)
+    back_step(0)
     lk.got(cot_x, g.cot_all.at[r_xn])
     cot_f = lk.put(g.cot_all.at[r_xn], g.cot_all.at[r_xn], sib)
-    gather_pass(up_g, up_region, 3)
-    for zl in range(2):
-        region = g.w_down_all.at[zl, 1 - y]
-        pltpu.make_async_copy(region, region, lk.recv_sems.at[dn_y + zl]).wait()
+    down_end()
     lk.got(cot_sib, g.cot_all.at[r_sib])
     lk.got(cot_f, g.cot_all.at[r_diag])
     down2d = g.w_down_all.reshape(768, 1024)
@@ -664,12 +711,14 @@
         return 0
 
     lax.fori_loop(0, 4, hidden_tile, 0)
+    up_step(3)
+    back_step(1)
     channel_back_got(mix_s, g.mix.at[r])
     mix_x = lk.put(g.mix.at[r], g.mix.at[r], xn)
     mix_sib = lk.put(g.mix.at[r], g.mix.at[r], sib)
-    gather_pass(back_g, back_region, 1)
-
-    gather_end(up_g, up_region)
+    back_step(2)
+
+    up_end()
     up2d = g.w_up_all.reshape(1024, 768)
 
     def up_tile(q, _):
@@ -681,13 +730,11 @@
         g.slope[rows, :] = gh * slope
         return 0
 
-    lax.fori_loop(0, 2, up_tile, 0)
-    gather_pass(back_g, back_region, 2)
-    lax.fori_loop(2, 4, up_tile, 0)
-    gather_pass(back_g, back_region, 3)
+    back_step(3)
+    lax.fori_loop(0, 4, up_tile, 0)
     lk.got(mix_x, g.mix.at[r_xn])
     mix_f = lk.put(g.mix.at[r_xn], g.mix.at[r_xn], sib)
-    gather_end(back_g, back_region)
+    back_end()
     back2d = g.w_back_all.reshape(512, 768)
 
     def mixed_part(ranks, q):
@@ -776,19 +823,41 @@
                 g.gd.at[zl, y, part], g.gd_in.at[z], lk.take(), gd_r + z, dev(x, z_d, y, cm), here
             )
 
+    other = pl.ds(aligned(64 * (1 - y), 64), 64)
+    own64 = pl.ds(aligned(64 * y, 64), 64)
+    up_y, gu_s = {}, {}
+
+    def up_grad(k):
+        z_d = zo(k)
+        rows = pl.ds(aligned(256 * z_d, 256), 256)
+        part = dot(g.normed_t[rows, :], g.g_up[...]).astype(bf16)
+        g.gu[z_d] = part.reshape(2, 128, 768)
+        up_y[k] = lk.put(g.gu.at[z_d, :, other], g.gu_y.at[z_d], ynb)
+
+    def up_sum(k):
+        z_d = zo(k)
+        lk.got(up_y[k], g.gu_y.at[z_d])
+        total = g.gu[z_d, :, own64, :].astype(f32) + g.gu_y[z_d].astype(f32)
+        g.gu[z_d, :, own64, :] = total.astype(bf16)
+        if k:
+            gu_s[k] = lk.put(g.gu.at[z_d, :, own64], g.gu_in.at[k - 1], dev(x, z_d, y, c))
+
+    up_grad(2)
+    up_grad(1)
+
     channel_got(gm_cs, g.gm_land)
     unpack(g.gm_land, put_grad)
     down_sum(0)
 
     def conv_back(h, _):
         parts = [conv_rows(h, k) for k in range(16)]
-        own = g.vr32[pl.ds(h, 64, stride=16), :].T.astype(bf16)
+        own = g.vr32[pl.ds(aligned(64 * h, 64), 64), :].T.astype(bf16)
         out = g.skip_b[pl.ds(16 * x + h, 1), :] * parts[0]
         lhs = []
         for kk in range(8):
             lhs.append(jnp.concatenate([parts[2 * kk], parts[2 * kk + 1]], axis=1).astype(bf16))
             out = out + dot(lhs[kk], g.toep[h, 2 * kk : 2 * kk + 2].reshape(256, 128))
-        g.o32[pl.ds(h, 64, stride=16), :] = out
+        g.o32[pl.ds(aligned(64 * h, 64), 64), :] = out
         after = jnp.zeros((128, 128), f32)
         for kk in range(7, -1, -1):
             pair = dot(own, lhs[kk])
@@ -807,30 +876,11 @@
     gv_s = channel_back(g.gv_out, g.g_val)
     g.g_val[pl.ds(aligned(16 * n, 16), 16), :] = g.gv_out[n]
 
-    other = pl.ds(aligned(64 * (1 - y), 64), 64)
-    own64 = pl.ds(aligned(64 * y, 64), 64)
-    up_y, gu_s = {}, {}
-
-    def up_grad(k):
-        z_d = zo(k)
-        rows = pl.ds(aligned(256 * z_d, 256), 256)
-        part = dot(g.normed_t[rows, :], g.g_up[...]).astype(bf16)
-        g.gu[z_d] = part.reshape(2, 128, 768)
-        up_y[k] = lk.put(g.gu.at[z_d, :, other], g.gu_y.at[z_d], ynb)
-
-    def up_sum(k):
-        z_d = zo(k)
-        lk.got(up_y[k], g.gu_y.at[z_d])
-        total = g.gu[z_d, :, own64, :].astype(f32) + g.gu_y[z_d].astype(f32)
-        g.gu[z_d, :, own64, :] = total.astype(bf16)
-        if k:
-            gu_s[k] = lk.put(g.gu.at[z_d, :, own64], g.gu_in.at[k - 1], dev(x, z_d, y, c))
-
-    up_grad(2)
-    up_grad(1)
+    down_sum(1)
+    up_sum(2)
     up_grad(3)
     up_grad(0)
-    down_sum(1)
+    up_sum(1)
 
     mix2d = g.mix.reshape(512, 1024)
 
@@ -904,8 +954,6 @@
     gn_s, gn_own = group_sum(
         normed_part, spare.at[1], g.gn_in, g.tok_all.at[r_sib].reshape(256, 1024), g.gn_xin
     )
-    up_sum(2)
-    up_sum(1)
     br_s, br_own = group_sum(
         branch_part, spare.at[0], g.br_in, g.tok_all.at[r].reshape(256, 1024), g.br_xin
     )
@@ -1015,9 +1063,6 @@
         lk.got(fin_u[i], g.fu_in.at[rm])
         lk.got(fin_b[i], g.fb_in.at[rm])
         lk.got(fin_v[i], g.fv_in.at[rm])
-    for rr in range(4):
-        g.o_up[:, 768 * rr : 768 * rr + 768] = g.fu_in[rr].astype(f32)
-        g.o_back[:, 768 * rr : 768 * rr + 768] = g.fb_in[rr].astype(f32)
     wide = jnp.concatenate([g.fv_in[rr] for rr in range(4)], axis=1)
     g.o_value[...] = dot_nt(wide, g.perm[...])
     for i in range(3):
@@ -1062,9 +1107,9 @@
         result=((2, 128, 1024), bf16),
         g_tokens=((2, 128, 1024), f32),
         o_norm=((8, 128), f32),
-        o_up=((32, 3072), f32),
+        fu_in=((4, 32, 768), bf16),
         o_value=((32, 512), f32),
-        o_back=((16, 3072), f32),
+        fb_in=((4, 16, 768), bf16),
         o_down=((96, 1024), f32),
         o_coef=((32, 512), f32),
         o_skip=((32, 128), f32),
@@ -1115,20 +1160,18 @@
         gu=((4, 2, 128, 768), bf16),
         gu_y=((4, 2, 64, 768), bf16),
         gu_in=((3, 2, 64, 768), bf16),
+        fv_in=((4, 32, 128), bf16),
         gu_f=((2, 2, 32, 768), bf16),
-        fu_in=((4, 32, 768), bf16),
         gb=((2, 2, 128, 768), bf16),
         gb_y=((2, 128, 768), bf16),
         gb_z=((4, 4, 16, 768), bf16),
         gb_in=((3, 4, 16, 768), bf16),
         gb_f=((4, 16, 768), bf16),
-        fb_in=((4, 16, 768), bf16),
         gv=((4, 2, 128, 128), bf16),
         gv_y=((4, 2, 64, 128), bf16),
         gv_z=((4, 2, 64, 128), bf16),
         gv_in=((3, 2, 64, 128), bf16),
         gv_f=((2, 2, 32, 128), bf16),
-        fv_in=((4, 32, 128), bf16),
         gk8=((2048, 128), f32),
         gm_own=((128, 1024), f32),
         skip_sum=((16, 128), f32),
@@ -1160,19 +1203,46 @@
             collective_id=0, has_side_effects=True, vmem_limit_bytes=64 << 20
         ),
     )(*ins.values())
-    o = types.SimpleNamespace(**dict(zip(outs, got)))
-    return (
-        o.result,
-        o.g_tokens,
-        o.o_norm[0, :32],
-        o.o_norm[2, :32],
-        o.o_up,
-        o.o_value,
-        o.o_back,
-        o.o_down,
-        o.o_coef,
-        o.o_skip[:, 127],
-    )
+    up_rows, back_rows = w_up.shape[0], w_back.shape[0]
+    final = [
+        jax.ShapeDtypeStruct((2, 128, 1024), bf16),
+        jax.ShapeDtypeStruct((2, 128, 1024), f32),
+        jax.ShapeDtypeStruct((1, 32), f32),
+        jax.ShapeDtypeStruct((1, 32), f32),
+        jax.ShapeDtypeStruct((up_rows, 3072), f32),
+        jax.ShapeDtypeStruct((up_rows, 512), f32),
+        jax.ShapeDtypeStruct((back_rows, 3072), f32),
+        jax.ShapeDtypeStruct((96, 1024), f32),
+        jax.ShapeDtypeStruct((32, 512), f32),
+        jax.ShapeDtypeStruct((1, 32), f32),
+    ]
+    out = pl.pallas_call(
+        last_kernel,
+        out_shape=final,
+        in_specs=[vmem] * len(outs),
+        out_specs=[vmem] * len(final),
+        compiler_params=pltpu.CompilerParams(vmem_limit_bytes=32 << 20),
+    )(*got)
+    return tuple(v.reshape(-1) if v.shape[0] == 1 else v for v in out)
+
+
+def last_kernel(*refs):
+    (result, g_tokens, norm, up, value, back, down, coef, skip), out = refs[:9], refs[9:]
+    out[0][...] = result[...]
+    out[1][...] = g_tokens[...]
+    out[2][...] = norm[0:1, 0:32]
+    out[3][...] = norm[2:3, 0:32]
+    for rr in range(4):
+        out[4][:, 768 * rr : 768 * rr + 768] = up[rr].astype(f32)
+        out[6][:, 768 * rr : 768 * rr + 768] = back[rr].astype(f32)
+    out[5][...] = value[...]
+    out[7][...] = down[...]
+    out[8][...] = coef[...]
+    same = lax.broadcasted_iota(jnp.int32, (32, 32), 0) == lax.broadcasted_iota(
+        jnp.int32, (32, 32), 1
+    )
+    column = jnp.broadcast_to(skip[:, 127:128], (32, 32))
+    out[9][...] = jnp.sum(jnp.where(same, column, 0.0), axis=0, keepdims=True)
 
 
 def run(tokens, *rest):

time: 181 us -> 162 us (0.90)
  Pallas kernels: 170 us -> 152 us
    pallas_call x1, Pallas kernels: 170 us -> 151 us  [fast_body(): pl.pallas_call(functools.partial(layer_kernel, names), out_shape=[jax.Sha...]
    unnamed x19 -> x18, local copies, waits for them, and re-layouts: 6.77 us -> 8.13 us
where the time goes in v3:
time: 162 us; the launch traced here: 161 us
  Pallas kernels  152 us (94%)
  local copies, waits for them, and re-layouts  8.13 us (5%)
    pallas_call x1, Pallas kernels, fast_body(): pl.pallas_call(functools.partial(layer_kernel, names), out_shape=[jax.Sha...  151 us
    unnamed x18, local copies, waits for them, and re-layouts  8.13 us

profile of v3, /device:TPU:0, one launch (start us, length us, event | category | flops | bytes accessed | tf_op | source)
XLA Modules:
  0.0 161.1 jit_solution(11714950630294145326)
XLA Ops:
  0.6 150.7 %shard_map.231 = (bf16[2,128,1024]{2,1,0:T(8,128)(2,1)}, f32[2,128,1024]{2,1,0:T(8,128)}, f32[8,128]{1,0:T(8,128)}, bf16[4,32,768]{2,1,0:T(8,128)(2,1)}, f32[32,...) custom-call(bf16[2,128,1024]{2,1,0:T(8,128)(2,1)} %refs_0_.1, ...), custom_call_target="tpu_custom_call" | custom-call | tf_op jit(solution)/shard_map/pallas_call | solution.py:1195
  151.4 0.0 copy-start.7
  151.4 0.7 copy-done.7
  152.1 0.0 copy-start
  152.1 1.2 copy-done
  153.3 0.0 copy-start.1
  153.3 1.0 copy-done.1
  154.3 0.0 copy-start.2
  154.3 1.0 copy-done.2
  155.3 0.0 copy-start.3
  155.3 0.9 copy-done.3
  156.3 0.0 copy-start.4
  156.3 0.9 copy-done.4
  157.2 0.0 copy-start.5
  157.2 0.8 copy-done.5
  158.0 0.0 copy-start.6
  158.0 0.8 copy-done.6
  158.8 0.0 copy-start.8
  158.8 0.7 copy-done.8
  159.5 1.6 shard_map.232
Async XLA Ops:
  151.4 0.7 copy-start.7
  152.1 1.2 copy-start
  153.3 1.0 copy-start.1
  154.3 1.0 copy-start.2
  155.3 0.9 copy-start.3
  156.3 0.9 copy-start.4
  157.2 0.8 copy-start.5
  158.0 0.8 copy-start.6
  158.8 0.7 copy-start.8

commit v4 on v3

--- a/solution.py
+++ b/solution.py
@@ -524,7 +524,6 @@
         )
     for k in (1, 2, 3):
         gather_pass(pk_g, pk_region, k)
-    down_step(1)
     ii = lax.broadcasted_iota(jnp.int32, (128, 128), 0)
     jj = lax.broadcasted_iota(jnp.int32, (128, 128), 1)
     flip = (ii + jj == 127).astype(bf16)
@@ -539,6 +538,7 @@
         return 0
 
     lax.fori_loop(0, 16, toeplitz, 0, unroll=2)
+    down_step(1)
 
     gather_end(pk_g, pk_region)
     e_i = lax.broadcasted_iota(jnp.int32, (128, 1024), 0)
@@ -590,7 +590,6 @@
     norm_block(lambda s_: g.tokens[s_], r)
     lk.got(tok_sib, g.tok_all.at[r_sib])
     norm_block(lambda s_: g.tok_all[r_sib, s_], r_sib)
-    down_step(2)
     lk.got(tok_x, g.tok_all.at[r_xn])
     tok_f = lk.put(g.tok_all.at[r_xn], g.tok_all.at[r_xn], sib)
     norm_block(lambda s_: g.tok_all[r_xn, s_], r_xn)
@@ -632,6 +631,7 @@
 
     val_s = channel_send(g.val, g.val_in)
     g.val_in[n] = g.val[pl.ds(aligned(16 * n, 16), 16), :]
+    down_step(2)
     for i, (to, xm, cm, rm) in enumerate(members):
         lk.got(up_s[i], g.w_up_all.at[xm, n, cm])
     up_step(0)
@@ -750,6 +750,20 @@
 
     lax.fori_loop(0, 2, gm_sib, 0)
     gm_s = lk.put(g.gm_send, g.gm_in, sib)
+    lk.got(mix_sib, g.mix.at[r_sib])
+    lk.got(mix_f, g.mix.at[r_diag])
+
+    mix2d = g.mix.reshape(512, 1024)
+
+    def back_tile(i, _):
+        at = pl.ds(aligned(384 * i, 128), 384)
+        part = dot(mix2d[...], g.g_gate[:, at]).astype(bf16)
+        g.gb[:, :, :, at] = part.reshape(2, 2, 128, 384)
+        return 0
+
+    lax.fori_loop(0, 2, back_tile, 0)
+    gb_y = lk.put(g.gb.at[:, 1 - y], g.gb_y, ynb)
+
 
     def gm_mine(q, _):
         at = pl.ds(aligned(512 * q, 128), 512)
@@ -763,8 +777,6 @@
     g.gm_x[...] = (g.gm_x[...].astype(f32) + g.gm_in[1 - x].astype(f32)).astype(bf16)
     gm_xs = lk.put(g.gm_x, g.gm_xin, xn)
 
-    lk.got(mix_sib, g.mix.at[r_sib])
-    lk.got(mix_f, g.mix.at[r_diag])
 
     def turn(i, _):
         rr, tb = i // 8, lax.rem(i, 8)
@@ -796,9 +808,12 @@
             return 0
 
         lax.fori_loop(0, 2, tile, 0)
+
+    def down_send(zl):
         gd_y.append(lk.put(g.gd.at[zl, 1 - y], g.gd_y.at[zl], ynb))
 
     down_grad(0)
+    down_grad(1)
 
     lk.got(gm_xs, g.gm_xin)
     for tb in range(8):
@@ -808,7 +823,8 @@
     gm_cs = channel_send(g.gm, g.gm_land)
     g.gm_land[n] = g.gm[pl.ds(aligned(16 * n, 16), 16), :]
 
-    down_grad(1)
+    down_send(0)
+
     gd_r = lk.take(4)
 
     def down_sum(zl):
@@ -823,6 +839,29 @@
                 g.gd.at[zl, y, part], g.gd_in.at[z], lk.take(), gd_r + z, dev(x, z_d, y, cm), here
             )
 
+    def group_sum(part, send, land, xsend, xland):
+        for xm in range(2):
+            send[xm] = part(xm, 1 - c).astype(bf16)
+        first = lk.put(send, land, sib)
+        mine = part(1 - x, c)
+        lk.got(first, land)
+        xsend[...] = (mine + land[1 - x].astype(f32)).astype(bf16)
+        second = lk.put(xsend, xland, xn)
+
+        def own():
+            return part(x, c) + land[x].astype(f32) + xland[...].astype(f32)
+
+        return second, own
+
+    def branch_part(xm, cm):
+        rows = pl.ds(aligned(256 * (2 * xm + cm), 256), 256)
+        return dot(g.hidden[rows, :], down2d[...])
+
+    spare = g.normed.reshape(2, 2, 256, 1024)
+    br_s, br_own = group_sum(
+        branch_part, spare.at[0], g.br_in, g.tok_all.at[r].reshape(256, 1024), g.br_xin
+    )
+
     other = pl.ds(aligned(64 * (1 - y), 64), 64)
     own64 = pl.ds(aligned(64 * y, 64), 64)
     up_y, gu_s = {}, {}
@@ -842,12 +881,15 @@
         if k:
             gu_s[k] = lk.put(g.gu.at[z_d, :, own64], g.gu_in.at[k - 1], dev(x, z_d, y, c))
 
-    up_grad(2)
-    up_grad(1)
-
+
+    lk.got(gb_y, g.gb_y)
+    total = g.gb[:, y].astype(f32) + g.gb_y[...].astype(f32)
+    g.gb_z[...] = total.astype(bf16).reshape(4, 4, 16, 768)
+    gb_s = {}
+    for k in (2, 1, 3):
+        gb_s[k] = lk.put(g.gb_z.at[:, zo(k)], g.gb_in.at[k - 1], dev(x, zo(k), y, c))
     channel_got(gm_cs, g.gm_land)
     unpack(g.gm_land, put_grad)
-    down_sum(0)
 
     def conv_back(h, _):
         parts = [conv_rows(h, k) for k in range(16)]
@@ -871,27 +913,16 @@
                 g.gk8[at, :] = jnp.sum(lag.reshape(16, 8, 128), axis=0)
         return 0
 
-    lax.fori_loop(0, 16, conv_back, 0)
+    lax.fori_loop(0, 8, conv_back, 0, unroll=2)
+    up_grad(2)
+    lax.fori_loop(8, 16, conv_back, 0, unroll=2)
     pack(g.gv_out, True)
     gv_s = channel_back(g.gv_out, g.g_val)
     g.g_val[pl.ds(aligned(16 * n, 16), 16), :] = g.gv_out[n]
 
-    down_sum(1)
+    down_send(1)
+    down_sum(0)
     up_sum(2)
-    up_grad(3)
-    up_grad(0)
-    up_sum(1)
-
-    mix2d = g.mix.reshape(512, 1024)
-
-    def back_tile(i, _):
-        at = pl.ds(aligned(384 * i, 128), 384)
-        part = dot(mix2d[...], g.g_gate[:, at]).astype(bf16)
-        g.gb[:, :, :, at] = part.reshape(2, 2, 128, 384)
-        return 0
-
-    lax.fori_loop(0, 2, back_tile, 0)
-    gb_y = lk.put(g.gb.at[:, 1 - y], g.gb_y, ynb)
 
     tall = g.gk8[pl.ds(0, 256, stride=8), :]
     for s_ in range(1, 8):
@@ -928,51 +959,28 @@
     g.gv[...] = part.reshape(4, 2, 128, 128)
     gv_y = lk.put(g.gv.at[:, :, other], g.gv_y, ynb)
 
-    def group_sum(part, send, land, xsend, xland):
-        for xm in range(2):
-            send[xm] = part(xm, 1 - c).astype(bf16)
-        first = lk.put(send, land, sib)
-        mine = part(1 - x, c)
-        lk.got(first, land)
-        xsend[...] = (mine + land[1 - x].astype(f32)).astype(bf16)
-        second = lk.put(xsend, xland, xn)
-
-        def own():
-            return part(x, c) + land[x].astype(f32) + xland[...].astype(f32)
-
-        return second, own
-
-    def branch_part(xm, cm):
-        rows = pl.ds(aligned(256 * (2 * xm + cm), 256), 256)
-        return dot(g.hidden[rows, :], down2d[...])
-
     def normed_part(xm, cm):
         rows = pl.ds(aligned(256 * (2 * xm + cm), 256), 256)
         return dot_nt(g.g_up[rows, :], up2d[...]) + dot_nt(g.gvp_t[rows, :], g.w_val[...])
 
-    spare = g.normed.reshape(2, 2, 256, 1024)
     gn_s, gn_own = group_sum(
         normed_part, spare.at[1], g.gn_in, g.tok_all.at[r_sib].reshape(256, 1024), g.gn_xin
     )
-    br_s, br_own = group_sum(
-        branch_part, spare.at[0], g.br_in, g.tok_all.at[r].reshape(256, 1024), g.br_xin
-    )
-    up_sum(3)
-    up_sum(0)
-
-    lk.got(gb_y, g.gb_y)
-    total = g.gb[:, y].astype(f32) + g.gb_y[...].astype(f32)
-    g.gb_z[...] = total.astype(bf16).reshape(4, 4, 16, 768)
-    gb_s = {}
-    for k in (2, 1, 3):
-        gb_s[k] = lk.put(g.gb_z.at[:, zo(k)], g.gb_in.at[k - 1], dev(x, zo(k), y, c))
+    up_grad(1)
+    up_grad(3)
+    up_grad(0)
+    down_sum(1)
+
     lk.got(gv_y, g.gv_y)
     g.gv_z[...] = (g.gv[:, :, own64, :].astype(f32) + g.gv_y[...].astype(f32)).astype(bf16)
     gv_zs = {}
     for k in (2, 1, 3):
         gv_zs[k] = lk.put(g.gv_z.at[zo(k)], g.gv_in.at[k - 1], dev(x, zo(k), y, c))
 
+    up_sum(1)
+
     lk.got(gn_s, g.gn_xin)
+    up_sum(3)
     g.state[...] = gn_own()
 
     def norm_back(i, carry):
@@ -1009,6 +1017,8 @@
     lk.got(br_s, g.br_xin)
     out = br_own().reshape(2, 128, 1024) + g.tokens[...].astype(f32)
     g.result[...] = out.astype(bf16)
+
+    up_sum(0)
 
     for k in (2, 1, 3):
         lk.got(gu_s[k], g.gu_in.at[k - 1])
@@ -1221,7 +1231,7 @@
         out_shape=final,
         in_specs=[vmem] * len(outs),
         out_specs=[vmem] * len(final),
-        compiler_params=pltpu.CompilerParams(vmem_limit_bytes=32 << 20),
+        compiler_params=pltpu.CompilerParams(vmem_limit_bytes=63 << 20),
     )(*got)
     return tuple(v.reshape(-1) if v.shape[0] == 1 else v for v in out)
 

time: 162 us -> 151 us (0.932)
  local copies, waits for them, and re-layouts: 8.13 us -> 0 us
  Pallas kernels: 152 us -> 150 us
    unnamed x18 -> x0, local copies, waits for them, and re-layouts: 8.13 us -> none
    pallas_call x1, Pallas kernels: 151 us -> 146 us  [fast_body(): pl.pallas_call(functools.partial(layer_kernel, names), out_shape=[jax.Sha...]
    pallas_call x1, Pallas kernels: 1.58 us -> 3.26 us  [fast_body(): pl.pallas_call(last_kernel, out_shape=final, in_specs=[vmem] * len(outs),...]
where the time goes in v4:
time: 151 us; the launch traced here: 150 us
  Pallas kernels  150 us (99%)
    pallas_call x1, Pallas kernels, fast_body(): pl.pallas_call(functools.partial(layer_kernel, names), out_shape=[jax.Sha...  146 us
    pallas_call x1, Pallas kernels, fast_body(): pl.pallas_call(last_kernel, out_shape=final, in_specs=[vmem] * len(outs),...  3.26 us

profile of v4, /device:TPU:0, one launch (start us, length us, event | category | flops | bytes accessed | tf_op | source)
XLA Modules:
  0.0 150.5 jit_solution(3051191439857133812)
XLA Ops:
  0.6 146.4 %shard_map.231 = (bf16[2,128,1024]{2,1,0:T(8,128)(2,1)}, f32[2,128,1024]{2,1,0:T(8,128)}, f32[8,128]{1,0:T(8,128)}, bf16[4,32,768]{2,1,0:T(8,128)(2,1)}, f32[32,...) custom-call(bf16[2,128,1024]{2,1,0:T(8,128)(2,1)} %refs_0_.1, ...), custom_call_target="tpu_custom_call" | custom-call | tf_op jit(solution)/shard_map/pallas_call | solution.py:1205
  147.1 3.3 %shard_map.232 = (bf16[2,128,1024]{2,1,0:T(8,128)(2,1)}, f32[2,128,1024]{2,1,0:T(8,128)}, f32[1,32]{1,0:T(1,128)}, f32[1,32]{1,0:T(1,128)}, f32[32,3072]{1,0:T(8...) custom-call(bf16[2,128,1024]{2,1,0:T(8,128)(2,1)} %get-tuple-element, ...), custom_call_target="tpu_custom_call" | custom-call | tf_op jit(solution)/shard_map/pallas_call | solution.py:1229

commit v5 on v4

--- a/solution.py
+++ b/solution.py
@@ -326,6 +326,12 @@
 N_SEMS = 200
 
 
+def channels_of(rr):
+    ch = lax.broadcasted_iota(jnp.int32, (512, 128), 0)
+    p = lax.broadcasted_iota(jnp.int32, (512, 128), 1)
+    return (ch == 64 * (p // 16) + 32 * (rr % 2) + 16 * (rr // 2) + p % 16).astype(bf16)
+
+
 def layer_kernel(names, *refs):
     r_ = dict(zip(names, refs))
     g = types.SimpleNamespace(**r_)
@@ -366,8 +372,6 @@
         jnp.int32, (32, 128), 1
     )
     eye = eye.astype(bf16)
-    ch_i = lax.broadcasted_iota(jnp.int32, (512, 128), 0)
-    p_i = lax.broadcasted_iota(jnp.int32, (512, 128), 1)
     row16 = lax.broadcasted_iota(jnp.int32, (16, 128), 0)
     gain_row = dot(g.norm_gain[...], eye)
     shift_row = dot(g.norm_shift[...], eye)
@@ -377,9 +381,7 @@
         jnp.where(row16 == 1, jnp.broadcast_to(shift_row, (16, 128)), 0.0),
     ).astype(bf16)
     for rr in range(4):
-        pick = ch_i == 64 * (p_i // 16) + 32 * (rr % 2) + 16 * (rr // 2) + p_i % 16
-        pick = pick.astype(bf16)
-        g.perm[:, 128 * rr : 128 * rr + 128] = pick
+        pick = channels_of(rr)
         g.pk_send[rr, 0:32, :] = dot(g.w_value[...], pick).astype(bf16)
         g.pk_send[rr, 32:48, :] = norm_pack
     pl.semaphore_wait(barrier, len(partners))
@@ -742,14 +744,12 @@
         w = w[0] if len(w) == 1 else jnp.concatenate(w, axis=0)
         return dot_nt(w, g.g_gate[pl.ds(aligned(512 * q, 512), 512), :])
 
-    def gm_sib(q, _):
-        at = pl.ds(aligned(512 * q, 128), 512)
+    gm_s, gm_xs = [], []
+    for q in range(2):
+        at = slice(512 * q, 512 * q + 512)
         both = mixed_part((1 - c, 2 + 1 - c), q).astype(bf16)
         g.gm_send[:, :, at] = both.reshape(2, 128, 512)
-        return 0
-
-    lax.fori_loop(0, 2, gm_sib, 0)
-    gm_s = lk.put(g.gm_send, g.gm_in, sib)
+        gm_s.append(lk.put(g.gm_send.at[:, :, at], g.gm_in.at[:, :, at], sib))
     lk.got(mix_sib, g.mix.at[r_sib])
     lk.got(mix_f, g.mix.at[r_diag])
 
@@ -765,17 +765,13 @@
     gb_y = lk.put(g.gb.at[:, 1 - y], g.gb_y, ynb)
 
 
-    def gm_mine(q, _):
-        at = pl.ds(aligned(512 * q, 128), 512)
+    for q in range(2):
+        at = slice(512 * q, 512 * q + 512)
         both = mixed_part((2 * (1 - x) + c, 2 * x + c), q)
-        g.gm_x[:, at] = both[0:128, :].astype(bf16)
-        g.gm_own[:, at] = both[128:256, :]
-        return 0
-
-    lax.fori_loop(0, 2, gm_mine, 0)
-    lk.got(gm_s, g.gm_in)
-    g.gm_x[...] = (g.gm_x[...].astype(f32) + g.gm_in[1 - x].astype(f32)).astype(bf16)
-    gm_xs = lk.put(g.gm_x, g.gm_xin, xn)
+        g.state[0:128, at] = both[128:256, :]
+        lk.got(gm_s[q], g.gm_in.at[:, :, at])
+        g.gm_x[:, at] = (both[0:128, :] + g.gm_in[1 - x, :, at].astype(f32)).astype(bf16)
+        gm_xs.append(lk.put(g.gm_x.at[:, at], g.gm_xin.at[:, at], xn))
 
 
     def turn(i, _):
@@ -815,29 +811,77 @@
     down_grad(0)
     down_grad(1)
 
-    lk.got(gm_xs, g.gm_xin)
     for tb in range(8):
+        if tb % 4 == 0:
+            half = slice(128 * tb, 128 * tb + 512)
+            lk.got(gm_xs[tb // 4], g.gm_xin.at[:, half])
         at = slice(128 * tb, 128 * tb + 128)
-        total = g.gm_own[:, at] + g.gm_in[x, :, at].astype(f32) + g.gm_xin[:, at].astype(f32)
-        g.gm[:, at] = dot(total.astype(bf16), flip).astype(bf16)
-    gm_cs = channel_send(g.gm, g.gm_land)
-    g.gm_land[n] = g.gm[pl.ds(aligned(16 * n, 16), 16), :]
+        total = g.state[0:128, at] + g.gm_in[x, :, at].astype(f32) + g.gm_xin[:, at].astype(f32)
+        g.w_val_t[:, at] = dot(total.astype(bf16), flip).astype(bf16)
+    gm_cs = channel_send(g.w_val_t, g.gm_land)
+    g.gm_land[n] = g.w_val_t[pl.ds(aligned(16 * n, 16), 16), :]
 
     down_send(0)
-
-    gd_r = lk.take(4)
+    down_send(1)
+
+    z1 = z + 1 - 2 * lax.rem(z, 2)
+    z2 = zo(2)
+    z3 = 3 - z
+
+    def put_add(mine, pair):
+        return (mine[...].astype(f32) + pair[...].astype(f32)).astype(bf16)
+
+    near_half = z // 2 == c
+    gd_r = lk.take(3)
+    d_pair = (lk.take(), lk.take())
+
+    def down_owner(zl, when, zd, place):
+        for cm in range(2):
+            src = g.gd.at[zl, y, pl.ds(96 * cm, 96)]
+            copy = lk.make(src, g.gd_in.at[place], lk.take(), gd_r + place, dev(x, zd, y, cm))
+            pl.when(when)(copy.start)
+            lk.pending.append((copy, when))
 
     def down_sum(zl):
         lk.got(gd_y[zl], g.gd_y.at[zl])
-        for cm in range(2):
-            part = pl.ds(96 * cm, 96)
-            total = g.gd[zl, y, part, :].astype(f32) + g.gd_y[zl, part, :].astype(f32)
-            g.gd[zl, y, part, :] = total.astype(bf16)
-            z_d = 2 * c + zl
-            here = jnp.logical_and(z_d == z, c == cm)
-            lk.put_or_keep(
-                g.gd.at[zl, y, part], g.gd_in.at[z], lk.take(), gd_r + z, dev(x, z_d, y, cm), here
-            )
+        total = g.gd[zl, y].astype(f32) + g.gd_y[zl].astype(f32)
+        g.gd[zl, y] = total.astype(bf16)
+        same = lax.rem(z, 2) == zl
+        down_owner(zl, jnp.logical_and(near_half, jnp.logical_not(same)), z1, 1)
+        copy = lk.make(g.gd.at[zl, y], g.gd_p, d_pair[zl], d_pair[zl], dev(x, z1, y, c))
+        sends = jnp.logical_and(jnp.logical_not(near_half), jnp.logical_not(same))
+        pl.when(sends)(copy.start)
+        lk.pending.append((copy, sends))
+        own = jnp.logical_and(near_half, same)
+
+        @pl.when(own)
+        def _():
+            g.gd_in[0] = g.gd[zl, y, pl.ds(aligned(96 * c, 32), 96), :]
+
+        other = g.gd.at[zl, y, pl.ds(aligned(96 * (1 - c), 32), 96)]
+        copy = lk.make(other, g.gd_in.at[0], lk.take(), gd_r, sib)
+        pl.when(own)(copy.start)
+        lk.pending.append((copy, own))
+
+    def down_far(zl):
+        adds = jnp.logical_and(jnp.logical_not(near_half), lax.rem(z, 2) == zl)
+
+        @pl.when(adds)
+        def _():
+            lk.make(g.gd_p, g.gd_p, d_pair[zl], d_pair[zl], ynb).wait_recv()
+            g.gd[zl, y] = put_add(g.gd.at[zl, y], g.gd_p)
+
+        down_owner(zl, adds, z2, 2)
+
+    def back_pairs():
+        near = lk.put(g.gb_z.at[:, z1], g.gb_in.at[0], dev(x, z1, y, c))
+        pair = lk.put(g.gb_z.at[:, z3], g.gb_in.at[1], dev(x, z1, y, c))
+        return near, pair
+
+    def back_far(pair):
+        lk.got(pair, g.gb_in.at[1])
+        g.gb_z[:, z2] = put_add(g.gb_z.at[:, z2], g.gb_in.at[1])
+        return lk.put(g.gb_z.at[:, z2], g.gb_in.at[2], dev(x, z2, y, c))
 
     def group_sum(part, send, land, xsend, xland):
         for xm in range(2):
@@ -865,29 +909,31 @@
     other = pl.ds(aligned(64 * (1 - y), 64), 64)
     own64 = pl.ds(aligned(64 * y, 64), 64)
     up_y, gu_s = {}, {}
+    up_to = {0: z, 1: z1, 2: z2, 3: z3}
 
     def up_grad(k):
-        z_d = zo(k)
+        z_d = up_to[k]
         rows = pl.ds(aligned(256 * z_d, 256), 256)
         part = dot(g.normed_t[rows, :], g.g_up[...]).astype(bf16)
         g.gu[z_d] = part.reshape(2, 128, 768)
         up_y[k] = lk.put(g.gu.at[z_d, :, other], g.gu_y.at[z_d], ynb)
 
     def up_sum(k):
-        z_d = zo(k)
+        z_d = up_to[k]
         lk.got(up_y[k], g.gu_y.at[z_d])
         total = g.gu[z_d, :, own64, :].astype(f32) + g.gu_y[z_d].astype(f32)
+        if k == 2:
+            lk.got(gu_s[3], g.gu_in.at[0])
+            total = total + g.gu_in[0].astype(f32)
         g.gu[z_d, :, own64, :] = total.astype(bf16)
         if k:
-            gu_s[k] = lk.put(g.gu.at[z_d, :, own64], g.gu_in.at[k - 1], dev(x, z_d, y, c))
-
+            to = dev(x, up_to[2 if k == 2 else 1], y, c)
+            gu_s[k] = lk.put(g.gu.at[z_d, :, own64], g.gu_in.at[(1, 2, 0)[k - 1]], to)
 
     lk.got(gb_y, g.gb_y)
     total = g.gb[:, y].astype(f32) + g.gb_y[...].astype(f32)
     g.gb_z[...] = total.astype(bf16).reshape(4, 4, 16, 768)
-    gb_s = {}
-    for k in (2, 1, 3):
-        gb_s[k] = lk.put(g.gb_z.at[:, zo(k)], g.gb_in.at[k - 1], dev(x, zo(k), y, c))
+    gb_near, gb_pair = back_pairs()
     channel_got(gm_cs, g.gm_land)
     unpack(g.gm_land, put_grad)
 
@@ -914,15 +960,15 @@
         return 0
 
     lax.fori_loop(0, 8, conv_back, 0, unroll=2)
-    up_grad(2)
     lax.fori_loop(8, 16, conv_back, 0, unroll=2)
     pack(g.gv_out, True)
     gv_s = channel_back(g.gv_out, g.g_val)
     g.g_val[pl.ds(aligned(16 * n, 16), 16), :] = g.gv_out[n]
 
-    down_send(1)
+    up_grad(3)
     down_sum(0)
-    up_sum(2)
+    gb_far = back_far(gb_pair)
+    down_sum(1)
 
     tall = g.gk8[pl.ds(0, 256, stride=8), :]
     for s_ in range(1, 8):
@@ -966,10 +1012,12 @@
     gn_s, gn_own = group_sum(
         normed_part, spare.at[1], g.gn_in, g.tok_all.at[r_sib].reshape(256, 1024), g.gn_xin
     )
+    up_grad(2)
     up_grad(1)
-    up_grad(3)
     up_grad(0)
-    down_sum(1)
+    up_sum(3)
+    down_far(0)
+    down_far(1)
 
     lk.got(gv_y, g.gv_y)
     g.gv_z[...] = (g.gv[:, :, own64, :].astype(f32) + g.gv_y[...].astype(f32)).astype(bf16)
@@ -977,10 +1025,10 @@
     for k in (2, 1, 3):
         gv_zs[k] = lk.put(g.gv_z.at[zo(k)], g.gv_in.at[k - 1], dev(x, zo(k), y, c))
 
+    up_sum(2)
+
+    lk.got(gn_s, g.gn_xin)
     up_sum(1)
-
-    lk.got(gn_s, g.gn_xin)
-    up_sum(3)
     g.state[...] = gn_own()
 
     def norm_back(i, carry):
@@ -1020,18 +1068,15 @@
 
     up_sum(0)
 
-    for k in (2, 1, 3):
-        lk.got(gu_s[k], g.gu_in.at[k - 1])
     total = g.gu[z, :, own64, :].astype(f32)
-    for k in range(3):
-        total = total + g.gu_in[k].astype(f32)
+    for k in (2, 1):
+        lk.got(gu_s[k], g.gu_in.at[(1, 2, 0)[k - 1]])
+        total = total + g.gu_in[(1, 2, 0)[k - 1]].astype(f32)
     g.gu_f[...] = total.reshape(2, 2, 32, 768).astype(bf16)
     fin_u = [lk.put(g.gu_f.at[xm, cm], g.fu_in.at[r], to) for to, xm, cm, rm in members]
-    for k in (2, 1, 3):
-        lk.got(gb_s[k], g.gb_in.at[k - 1])
-    total = g.gb_z[:, z].astype(f32)
-    for k in range(3):
-        total = total + g.gb_in[k].astype(f32)
+    lk.got(gb_near, g.gb_in.at[0])
+    lk.got(gb_far, g.gb_in.at[2])
+    total = g.gb_z[:, z].astype(f32) + g.gb_in[0].astype(f32) + g.gb_in[2].astype(f32)
     g.gb_f[...] = total.astype(bf16)
     fin_b = [lk.put(g.gb_f.at[2 * cm + xm], g.fb_in.at[r], to) for to, xm, cm, rm in members]
     for k in (2, 1, 3):
@@ -1045,13 +1090,18 @@
     g.fb_in[r] = g.gb_f[2 * c + x]
     g.fv_in[r] = g.gv_f[x, c]
 
-    for zs in range(4):
-        region = g.gd_in.at[zs]
-        pltpu.make_async_copy(region, region, lk.recv_sems.at[gd_r + zs]).wait()
-    total = g.gd_in[0].astype(f32)
-    for zs in range(1, 4):
-        total = total + g.gd_in[zs].astype(f32)
-    g.o_down[...] = total
+    from_sib = owner != c
+
+    @pl.when(from_sib)
+    def _():
+        lk.make(g.gd_in.at[0], g.gd_in.at[0], gd_r, gd_r, sib).wait_recv()
+
+    for place in (1, 2):
+        region = g.gd_in.at[place]
+        lk.make(region, region, gd_r + place, gd_r + place, sib).wait_recv()
+    g.o_down[...] = (
+        g.gd_in[0].astype(f32) + g.gd_in[1].astype(f32) + g.gd_in[2].astype(f32)
+    )
 
     mine = pl.ds(aligned(16 * x, 16), 16)
     theirs = pl.ds(aligned(16 * (1 - x), 16), 16)
@@ -1073,8 +1123,6 @@
         lk.got(fin_u[i], g.fu_in.at[rm])
         lk.got(fin_b[i], g.fb_in.at[rm])
         lk.got(fin_v[i], g.fv_in.at[rm])
-    wide = jnp.concatenate([g.fv_in[rr] for rr in range(4)], axis=1)
-    g.o_value[...] = dot_nt(wide, g.perm[...])
     for i in range(3):
         lk.got(ng_t[i], g.ng_fin.at[i])
         total = total + g.ng_fin[i]
@@ -1118,14 +1166,13 @@
         g_tokens=((2, 128, 1024), f32),
         o_norm=((8, 128), f32),
         fu_in=((4, 32, 768), bf16),
-        o_value=((32, 512), f32),
+        fv_in=((4, 32, 128), bf16),
         fb_in=((4, 16, 768), bf16),
         o_down=((96, 1024), f32),
         o_coef=((32, 512), f32),
         o_skip=((32, 128), f32),
     )
     scratch = dict(
-        perm=((512, 512), bf16),
         pk_send=((4, 48, 128), bf16),
         pk=((2, 8, 2, 48, 128), bf16),
         coef=((2, 16, 512), bf16),
@@ -1158,7 +1205,6 @@
         gm_in=((2, 128, 1024), bf16),
         gm_x=((128, 1024), bf16),
         gm_xin=((128, 1024), bf16),
-        gm=((128, 1024), bf16),
         gm_land=((8, 16, 1024), bf16),
         mix_tok=((1024, 512), bf16),
         hidden=((1024, 768), bf16),
@@ -1166,11 +1212,11 @@
         g_up=((1024, 768), bf16),
         gd=((2, 2, 192, 1024), bf16),
         gd_y=((2, 192, 1024), bf16),
-        gd_in=((4, 96, 1024), bf16),
+        gd_in=((3, 96, 1024), bf16),
+        gd_p=((192, 1024), bf16),
         gu=((4, 2, 128, 768), bf16),
         gu_y=((4, 2, 64, 768), bf16),
         gu_in=((3, 2, 64, 768), bf16),
-        fv_in=((4, 32, 128), bf16),
         gu_f=((2, 2, 32, 768), bf16),
         gb=((2, 2, 128, 768), bf16),
         gb_y=((2, 128, 768), bf16),
@@ -1183,7 +1229,6 @@
         gv_in=((3, 2, 64, 128), bf16),
         gv_f=((2, 2, 32, 128), bf16),
         gk8=((2048, 128), f32),
-        gm_own=((128, 1024), f32),
         skip_sum=((16, 128), f32),
         skip_in=((16, 128), f32),
         gcoef=((2, 16, 512), f32),
@@ -1245,7 +1290,7 @@
     for rr in range(4):
         out[4][:, 768 * rr : 768 * rr + 768] = up[rr].astype(f32)
         out[6][:, 768 * rr : 768 * rr + 768] = back[rr].astype(f32)
-    out[5][...] = value[...]
+    out[5][...] = sum(dot_nt(value[rr], channels_of(rr)) for rr in range(4))
     out[7][...] = down[...]
     out[8][...] = coef[...]
     same = lax.broadcasted_iota(jnp.int32, (32, 32), 0) == lax.broadcasted_iota(

time: 151 us -> 147 us (0.974)
  Pallas kernels: 150 us -> 146 us
    pallas_call x1, Pallas kernels: 146 us -> 143 us  [fast_body(): pl.pallas_call(functools.partial(layer_kernel, names), out_shape=[jax.Sha...]
where the time goes in v5:
time: 147 us
  Pallas kernels  146 us (99%)
    pallas_call x1, Pallas kernels, fast_body(): pl.pallas_call(functools.partial(layer_kernel, names), out_shape=[jax.Sha...  143 us
    pallas_call x1, Pallas kernels, fast_body(): pl.pallas_call(last_kernel, out_shape=final, in_specs=[vmem] * len(outs),...  3.4 us

profile of v5, /device:TPU:0, one launch (start us, length us, event | category | flops | bytes accessed | tf_op | source)
XLA Modules:
  0.0 146.8 jit_solution(1208294956347746070)
XLA Ops:
  0.6 142.6 %shard_map.231 = (bf16[2,128,1024]{2,1,0:T(8,128)(2,1)}, f32[2,128,1024]{2,1,0:T(8,128)}, f32[8,128]{1,0:T(8,128)}, bf16[4,32,768]{2,1,0:T(8,128)(2,1)}, bf16[4,...) custom-call(bf16[2,128,1024]{2,1,0:T(8,128)(2,1)} %refs_0_.1, ...), custom_call_target="tpu_custom_call" | custom-call | tf_op jit(solution)/shard_map/pallas_call | solution.py:1250
  143.3 3.4 %shard_map.232 = (bf16[2,128,1024]{2,1,0:T(8,128)(2,1)}, f32[2,128,1024]{2,1,0:T(8,128)}, f32[1,32]{1,0:T(1,128)}, f32[1,32]{1,0:T(1,128)}, f32[32,3072]{1,0:T(8...) custom-call(bf16[2,128,1024]{2,1,0:T(8,128)(2,1)} %get-tuple-element, ...), custom_call_target="tpu_custom_call" | custom-call | tf_op jit(solution)/shard_map/pallas_call | solution.py:1274

commit v6 on v5

--- a/solution.py
+++ b/solution.py
@@ -911,11 +911,14 @@
     up_y, gu_s = {}, {}
     up_to = {0: z, 1: z1, 2: z2, 3: z3}
 
-    def up_grad(k):
+    def up_part(k):
         z_d = up_to[k]
         rows = pl.ds(aligned(256 * z_d, 256), 256)
         part = dot(g.normed_t[rows, :], g.g_up[...]).astype(bf16)
         g.gu[z_d] = part.reshape(2, 128, 768)
+
+    def up_grad(k):
+        z_d = up_to[k]
         up_y[k] = lk.put(g.gu.at[z_d, :, other], g.gu_y.at[z_d], ynb)
 
     def up_sum(k):
@@ -934,6 +937,8 @@
     total = g.gb[:, y].astype(f32) + g.gb_y[...].astype(f32)
     g.gb_z[...] = total.astype(bf16).reshape(4, 4, 16, 768)
     gb_near, gb_pair = back_pairs()
+    for k in (3, 2, 1, 0):
+        up_part(k)
     channel_got(gm_cs, g.gm_land)
     unpack(g.gm_land, put_grad)
 
@@ -1027,6 +1032,17 @@
 
     up_sum(2)
 
+    lk.got(br_s, g.br_xin)
+    out = br_own().reshape(2, 128, 1024) + g.tokens[...].astype(f32)
+    g.result[...] = out.astype(bf16)
+
+    lk.got(gb_near, g.gb_in.at[0])
+    lk.got(gb_far, g.gb_in.at[2])
+    total = g.gb_z[:, z].astype(f32) + g.gb_in[0].astype(f32) + g.gb_in[2].astype(f32)
+    g.gb_f[...] = total.astype(bf16)
+    fin_b = [lk.put(g.gb_f.at[2 * cm + xm], g.fb_in.at[r], to) for to, xm, cm, rm in members]
+    g.fb_in[r] = g.gb_f[2 * c + x]
+
     lk.got(gn_s, g.gn_xin)
     up_sum(1)
     g.state[...] = gn_own()
@@ -1062,10 +1078,6 @@
         to = lax.rem(n + k, 8)
         ng_s.append(lk.put(g.ng.at[to // 2], g.ng_in.at[k - 1], (x, 2 * to + c)))
 
-    lk.got(br_s, g.br_xin)
-    out = br_own().reshape(2, 128, 1024) + g.tokens[...].astype(f32)
-    g.result[...] = out.astype(bf16)
-
     up_sum(0)
 
     total = g.gu[z, :, own64, :].astype(f32)
@@ -1074,11 +1086,6 @@
         total = total + g.gu_in[(1, 2, 0)[k - 1]].astype(f32)
     g.gu_f[...] = total.reshape(2, 2, 32, 768).astype(bf16)
     fin_u = [lk.put(g.gu_f.at[xm, cm], g.fu_in.at[r], to) for to, xm, cm, rm in members]
-    lk.got(gb_near, g.gb_in.at[0])
-    lk.got(gb_far, g.gb_in.at[2])
-    total = g.gb_z[:, z].astype(f32) + g.gb_in[0].astype(f32) + g.gb_in[2].astype(f32)
-    g.gb_f[...] = total.astype(bf16)
-    fin_b = [lk.put(g.gb_f.at[2 * cm + xm], g.fb_in.at[r], to) for to, xm, cm, rm in members]
     for k in (2, 1, 3):
         lk.got(gv_zs[k], g.gv_in.at[k - 1])
     total = g.gv_z[z].astype(f32)
@@ -1087,7 +1094,6 @@
     g.gv_f[...] = total.reshape(2, 2, 32, 128).astype(bf16)
     fin_v = [lk.put(g.gv_f.at[xm, cm], g.fv_in.at[r], to) for to, xm, cm, rm in members]
     g.fu_in[r] = g.gu_f[x, c]
-    g.fb_in[r] = g.gb_f[2 * c + x]
     g.fv_in[r] = g.gv_f[x, c]
 
     from_sib = owner != c

time: 147 us -> 144 us (0.980)
  Pallas kernels: 146 us -> 143 us
    pallas_call x1, Pallas kernels: 143 us -> 140 us  [fast_body(): pl.pallas_call(functools.partial(layer_kernel, names), out_shape=[jax.Sha...]
where the time goes in v6:
time: 144 us
  Pallas kernels  143 us (99%)
    pallas_call x1, Pallas kernels, fast_body(): pl.pallas_call(functools.partial(layer_kernel, names), out_shape=[jax.Sha...  140 us
    pallas_call x1, Pallas kernels, fast_body(): pl.pallas_call(last_kernel, out_shape=final, in_specs=[vmem] * len(outs),...  3.4 us

profile of v6, /device:TPU:0, one launch (start us, length us, event | category | flops | bytes accessed | tf_op | source)
XLA Modules:
  0.0 144.2 jit_solution(330686578531110673)
XLA Ops:
  0.6 140.1 %shard_map.231 = (bf16[2,128,1024]{2,1,0:T(8,128)(2,1)}, f32[2,128,1024]{2,1,0:T(8,128)}, f32[8,128]{1,0:T(8,128)}, bf16[4,32,768]{2,1,0:T(8,128)(2,1)}, bf16[4,...) custom-call(bf16[2,128,1024]{2,1,0:T(8,128)(2,1)} %refs_0_.1, ...), custom_call_target="tpu_custom_call" | custom-call | tf_op jit(solution)/shard_map/pallas_call | solution.py:1256
  140.7 3.4 %shard_map.232 = (bf16[2,128,1024]{2,1,0:T(8,128)(2,1)}, f32[2,128,1024]{2,1,0:T(8,128)}, f32[1,32]{1,0:T(1,128)}, f32[1,32]{1,0:T(1,128)}, f32[32,3072]{1,0:T(8...) custom-call(bf16[2,128,1024]{2,1,0:T(8,128)(2,1)} %get-tuple-element, ...), custom_call_target="tpu_custom_call" | custom-call | tf_op jit(solution)/shard_map/pallas_call | solution.py:1280
